TPU v7x, 1024 devices: a whole 4x8x16 slice. The times are simulated.
1024 devices in a mesh: dp: 64 (over x, z), expert: 16 (over y, core).
Axes of the slice: x: 4, y: 8, z: 16, core: 2. Of those that a mesh axis runs over, the one named last changes fastest.
Arguments:
- out_grad: bfloat16 [131072, 1440], P(('dp', 'expert')), may hold values from -0.022094727 to 0.022094727
- routes: int32 [131072, 4], P(('dp', 'expert')), may hold values from 0 to 3, as said below
- slots: int32 [131072, 4], P(('dp', 'expert')), may hold values from 0 to 127, as said below
- combine_weight: bfloat16 [131072, 4], P(('dp', 'expert')), may hold values from 0.049804688 to 1
- saved_hidden: bfloat16 [64, 16, 16, 128, 360], P('dp', 'expert'), may hold values from -6 to 6
- saved_out: bfloat16 [64, 16, 16, 128, 360], P('dp', 'expert'), may hold values from -12 to 12
Outputs:
- weight_grad: bfloat16 [16, 518400], P('expert', 'dp')
- router_grad: float32 [131072, 4], P(('dp', 'expert'))
Inputs may be any that keep to these rules, and one draw needn't show every extreme that they name: Each token names 4 different experts; the routes of one device name each expert at most 128 times and some expert exactly 128 times. The routes of one device to one expert hold distinct slots, from 0 up to their number minus one.
All inputs are finite; a program needn't handle non-finite values.
Results may differ from a plain program's by a relative error of at most 0.0049.
Values may be sent and summed in bfloat16 or wider, within the bound.
No kernel may reach another device: no remote copies, remote signals or barrier semaphores. Data moves between devices by JAX's collectives and lax.ppermute only.
A program may use at most 64 MiB of HBM per device.

v0:
```python
import jax
import jax.numpy as jnp
from jax import lax
from jax.sharding import PartitionSpec as P

FF = 1440


def local(out_grad, routes, slots, combine_weight, saved_hidden, saved_out):
    split_count = FF // saved_hidden.shape[4]
    devices = lax.axis_size("expert")
    experts = devices // split_count
    capacity = saved_hidden.shape[3]
    hidden_units = saved_hidden.shape[4]
    part_width = saved_out.shape[4]
    feature_count = out_grad.shape[1]
    cell_count = experts * capacity
    total_cells = devices * capacity
    cell_index = routes * capacity + slots
    matches = cell_index[:, :, None] == jnp.arange(cell_count, dtype=jnp.int32)[None, None, :]
    placed = jnp.sum(matches.astype(jnp.int32), axis=1).astype(jnp.bfloat16)
    outgoing = jnp.einsum("tc,td->cd", placed, out_grad, preferred_element_type=jnp.float32).astype(
        jnp.bfloat16
    )
    weight_cells = jnp.sum(
        jnp.where(matches, combine_weight[:, :, None].astype(jnp.float32), 0.0), axis=(0, 1)
    )
    sent_rows = jnp.repeat(outgoing.reshape(experts, capacity, feature_count), split_count, axis=0)
    sent_weights = jnp.repeat(
        weight_cells.astype(jnp.bfloat16).reshape(experts, capacity), split_count, axis=0
    )
    received, weights = (
        lax.all_to_all(sent_rows, "expert", split_axis=0, concat_axis=0, tiled=True),
        lax.all_to_all(sent_weights, "expert", split_axis=0, concat_axis=0, tiled=True),
    )
    arrived = received.reshape(total_cells, feature_count)
    arrived_weights = weights.reshape(total_cells)
    hidden_block = lax.axis_index("expert") % split_count
    arrived_part = lax.dynamic_slice_in_dim(arrived, hidden_block * part_width, part_width, 1)
    hidden_rows = saved_hidden.reshape(total_cells, hidden_units)
    output_rows = saved_out.reshape(total_cells, part_width)
    scores = jnp.einsum("rd,rd->r", output_rows, arrived_part, preferred_element_type=jnp.float32)
    scaled = (
        arrived_weights.reshape(total_cells, 1).astype(jnp.float32) * arrived.astype(jnp.float32)
    ).astype(jnp.bfloat16)
    returned = lax.all_to_all(
        scores.reshape(devices, capacity), "expert", split_axis=0, concat_axis=0, tiled=True
    )
    combined = jnp.sum(returned.reshape(experts, split_count, capacity), axis=1).reshape(cell_count)
    router_grad = jnp.sum(jnp.where(matches, combined[None, None, :], 0.0), axis=2)
    weight_term = jnp.einsum("rf,rd->fd", hidden_rows, scaled, preferred_element_type=jnp.float32)
    flat_term = weight_term.reshape(hidden_units * feature_count)
    summed = lax.psum_scatter(flat_term, "dp", scatter_dimension=0, tiled=True)
    weight_grad = summed.astype(jnp.bfloat16).reshape(1, summed.shape[0])
    return (weight_grad, router_grad)


def solution(mesh):
    return jax.shard_map(
        local,
        mesh=mesh,
        in_specs=(
            P(("dp", "expert"), None),
            P(("dp", "expert"), None),
            P(("dp", "expert"), None),
            P(("dp", "expert"), None),
            P("dp", "expert", None, None, None),
            P("dp", "expert", None, None, None),
        ),
        out_specs=(P("expert", "dp"), P(("dp", "expert"), None)),
        check_vma=False,
    )
```

profile of v0, /device:TPU:8, one launch (start us, length us, event | category | flops | bytes accessed | tf_op | source)
XLA Modules:
  0.0 499.8 jit_solution(163527489825569649)
XLA Ops:
  0.6 0.0 copy-start
  0.6 0.8 multiply_add_fusion
  1.4 0.2 convert_reduce_fusion
  1.6 0.1 copy-done
  1.7 0.5 fusion.10
  2.2 0.3 copy.69
  2.5 3.4 broadcast_in_dim.36
  5.8 0.0 copy-start.1
  5.8 17.6 %all-to-all-start.1 = ((bf16[16,128,1440]{1,2,0:T(8,128)(2,1)}), bf16[16,128,1440]{1,2,0:T(8,128)(2,1)}, u32[]{:S(2)}, u32[]{:S(2)}) async-start(bf16[16,128,1440]{1,2,0:T(8,128)(2,1)} %bitcast.45), calls=%async_computation.1 | async-start | bytes 11796480 | tf_op jit(solution)/shard_map/all_to_all | solution.py:33
  23.4 0.0 copy-done.1
  23.4 0.2 copy.45
  23.6 128.8 %all-to-all-done.1 = bf16[16,128,1440]{1,2,0:T(8,128)(2,1)} async-done(((bf16[16,128,1440]{1,2,0:T(8,128)(2,1)}), bf16[16,128,1440]{1,2,0:T(8,128)(2,1)}, u32[]{:S(2)}, u32[]{:S(2)}) %all-to-all-start.1) | async-done | bytes 5898272 | tf_op jit(solution)/shard_map/all_to_all | solution.py:33
  152.4 3.5 copy_bitcast_fusion
  155.9 0.0 copy-start.3
  155.9 0.0 copy-start.2
  155.9 1.3 fusion.7
  157.2 6.6 %all-to-all-start.2 = ((f32[16,1,128]{2,1,0:T(1,128)}), f32[16,1,128]{2,1,0:T(1,128)S(1)}, u32[]{:S(2)}, u32[]{:S(2)}) async-start(f32[16,1,128]{2,1,0:T(1,128)} %bitcast.5), calls=%async_computation.2 | async-start | bytes 16384 | tf_op jit(solution)/shard_map/all_to_all | solution.py:46
  163.8 0.0 copy-done.3
  163.8 6.1 %all-to-all-done.2 = f32[16,1,128]{2,1,0:T(1,128)S(1)} async-done(((f32[16,1,128]{2,1,0:T(1,128)}), f32[16,1,128]{2,1,0:T(1,128)S(1)}, u32[]{:S(2)}, u32[]{:S(2)}) %all-to-all-start.2) | async-done | bytes 8224 | tf_op jit(solution)/shard_map/all_to_all | solution.py:46
  170.0 1.0 select_reduce_fusion
  171.0 0.6 copy.39
  171.6 4.7 all-to-all-start
  176.3 0.0 copy-done.2
  176.3 0.2 copy.42
  176.5 1.4 dynamic-slice
  178.6 3.9 all-to-all-done
  182.5 7.3 %fusion.4 = f32[360,1440]{0,1:T(8,128)} fusion(bf16[45,8,16,128]{3,2,1,0:T(8,128)(2,1)S(1)} %bitcast.48, bf16[16,128,1440]{1,2,0:T(8,128)(2,1)} %all-to-all-done.1, f32[16,128]{1,0:T(8,128)S(1)} %bitcast.51), kind=kOutput, calls=%fused_computation.6 | convolution fusion | flops 2132213760 | bytes 9454592 | tf_op jit(solution)/shard_map/rf,rd->fd/dot_general | solution.py:51
  189.8 2.0 copy.43
  191.8 2.8 reshape.63
  194.6 304.4 %all-reduce.2 = bf16[518400]{0:T(1024)(128)(2,1)S(1)} all-reduce(f32[518400]{0:T(1024)} %reshape.63), channel_id=2, replica_groups=mesh['dp'=64,'expert'=16] {'dp'}, use_global_device_ids=true, to_apply=%region_2.3.clone | all-reduce | flops 518400 | bytes 3110400
  499.1 0.1 dynamic-slice.3
  499.2 0.6 reshape.64
  (4 shorter events, 0.0 us)
Async XLA Ops:
  0.6 1.0 copy-start
  5.8 17.6 %copy-start.1 = (bf16[1,1,16,128,360]{3,4,2,1,0:T(8,128)(2,1)S(1)}, bf16[1,1,16,128,360]{3,4,2,1,0:T(8,128)(2,1)}, u32[]{:S(2)}) copy-start(bf16[1,1,16,128,360]{3,4,2,1,0:T(8,128)(2,1)} %param.11) | copy-start | bytes 4423684
  5.8 146.6 %all-to-all-start.1 = ((bf16[16,128,1440]{1,2,0:T(8,128)(2,1)}), bf16[16,128,1440]{1,2,0:T(8,128)(2,1)}, u32[]{:S(2)}, u32[]{:S(2)}) async-start(bf16[16,128,1440]{1,2,0:T(8,128)(2,1)} %bitcast.45), calls=%async_computation.1 | async-start | bytes 11796480 | tf_op jit(solution)/shard_map/all_to_all | solution.py:33
  155.9 7.9 %copy-start.3 = (bf16[128,4]{0,1:T(4,128)(2,1)S(1)}, bf16[128,4]{0,1:T(4,128)(2,1)}, u32[]{:S(2)}) copy-start(bf16[128,4]{0,1:T(4,128)(2,1)} %param.9) | copy-start | bytes 3076
  155.9 20.4 %copy-start.2 = (bf16[1,1,16,128,360]{3,4,2,1,0:T(8,128)(2,1)S(1)}, bf16[1,1,16,128,360]{3,4,2,1,0:T(8,128)(2,1)}, u32[]{:S(2)}) copy-start(bf16[1,1,16,128,360]{3,4,2,1,0:T(8,128)(2,1)} %param.10) | copy-start | bytes 4423684
  157.2 12.8 %all-to-all-start.2 = ((f32[16,1,128]{2,1,0:T(1,128)}), f32[16,1,128]{2,1,0:T(1,128)S(1)}, u32[]{:S(2)}, u32[]{:S(2)}) async-start(f32[16,1,128]{2,1,0:T(1,128)} %bitcast.5), calls=%async_computation.2 | async-start | bytes 16384 | tf_op jit(solution)/shard_map/all_to_all | solution.py:46
  171.6 10.9 %all-to-all-start = ((bf16[16,1,128]{2,1,0:T(2,128)(2,1)}), bf16[16,1,128]{2,1,0:T(2,128)(2,1)S(1)}, u32[]{:S(2)}, u32[]{:S(2)}) async-start(bf16[16,1,128]{2,1,0:T(2,128)(2,1)} %copy.39), calls=%async_computation | async-start | bytes 16384 | tf_op jit(solution)/shard_map/all_to_all | solution.py:34
where the time goes:
time: 500 us
  blocking collectives  304 us (61%)
  waiting for transfers between devices  139 us (28%)
  starting transfers between devices  29 us (6%)
  local copies, waits for them, and re-layouts  15.1 us (3%)
  matrix products  7.82 us (2%)
    unnamed x1, blocking collectives  304 us
    all_to_all x1, waiting for transfers between devices, local(): lax.all_to_all(sent_rows, 'expert', split_axis=0, concat_axis=0, tiled=True)  129 us
    all_to_all x1, starting transfers between devices, local(): lax.all_to_all(sent_rows, 'expert', split_axis=0, concat_axis=0, tiled=True)  17.6 us
  transfers between devices with their start and end apart: 3, of which 3 were waited for; matrix products, arithmetic and copies ran while one was open for 0% of the time, Pallas kernels for 0%

commit v1 on v0

v1 whole, which is shorter than its diff:
```python
import jax
import jax.numpy as jnp
from jax import lax
from jax.experimental import pallas as pl
from jax.experimental.pallas import tpu as pltpu
from jax.sharding import Mesh, PartitionSpec as P

F32 = jnp.float32
BF16 = jnp.bfloat16
META = 16
PAIR = 2


def compute_kernel(where_ref, g_ref, h_ref, o_ref, w_ref, s_ref, acc):
    step = pl.program_id(0)
    expert = where_ref[0]
    part = where_ref[1]
    odd = lax.rem(part, 2)
    cols = g_ref.shape[1] - META
    units, cap = h_ref.shape[1:]
    groups, rows, _ = w_ref.shape
    live = units // groups
    width = o_ref.shape[1]
    pad = 8
    meta_row = lax.broadcasted_iota(jnp.int32, (META, cap), 0)
    slot_row = lax.broadcasted_iota(jnp.int32, (cap, cap), 0)
    lhs, rhs = [], []
    for u in range(PAIR):
        meta = g_ref[u, cols:, :].astype(F32)
        slot = jnp.sum(jnp.where(meta_row == expert, meta, 0.0), axis=0, keepdims=True)
        weight = jnp.sum(jnp.where(meta_row == expert + 4, meta, 0.0), axis=0, keepdims=True)
        place = (slot_row == slot.astype(jnp.int32)).astype(BF16)
        hidden = jnp.dot(h_ref[u], place, preferred_element_type=F32)
        out = jnp.dot(o_ref[u], place, preferred_element_type=F32)
        gap = jnp.zeros((pad, cap), F32)
        shifted = jnp.where(
            odd == 1, jnp.concatenate([gap, out], axis=0), jnp.concatenate([out, gap], axis=0)
        )
        start = pl.multiple_of(part * width - pad * odd, 16)
        window = g_ref[u, pl.ds(start, width + pad), :].astype(F32)
        s_ref[0, u : u + 1, :] = jnp.sum(shifted * window, axis=0, keepdims=True)
        blank = jnp.zeros((rows - live, cap), F32)
        spread = []
        for q in range(groups):
            spread += [hidden[q * live : (q + 1) * live], blank]
        lhs.append(jnp.concatenate(spread, axis=0).astype(BF16))
        rhs.append((g_ref[u, :cols, :].astype(F32) * weight).astype(BF16))
    term = lax.dot_general(
        jnp.concatenate(lhs, axis=1),
        jnp.concatenate(rhs, axis=1),
        (((1,), (1,)), ((), ())),
        preferred_element_type=F32,
    )

    @pl.when(step == 0)
    def _():
        acc[...] = term

    @pl.when(step > 0)
    def _():
        acc[...] += term

    @pl.when(step == pl.num_programs(0) - 1)
    def _():
        for q in range(groups):
            w_ref[q] = acc[q * rows : (q + 1) * rows, :].astype(BF16)


def compute(where, g, h, o, groups):
    sources, wide, cap = g.shape
    units = h.shape[1]
    cols = wide - META
    rows = -(-(units // groups) // 16) * 16
    return pl.pallas_call(
        compute_kernel,
        grid_spec=pltpu.PrefetchScalarGridSpec(
            num_scalar_prefetch=1,
            grid=(sources // PAIR,),
            in_specs=[
                pl.BlockSpec((PAIR, wide, cap), lambda i, w: (i, 0, 0)),
                pl.BlockSpec((PAIR, units, cap), lambda i, w: (i, 0, 0)),
                pl.BlockSpec((PAIR, o.shape[1], cap), lambda i, w: (i, 0, 0)),
            ],
            out_specs=[
                pl.BlockSpec((groups, rows, cols), lambda i, w: (0, 0, 0)),
                pl.BlockSpec((1, PAIR, cap), lambda i, w: (i, 0, 0)),
            ],
            scratch_shapes=[pltpu.VMEM((groups * rows, cols), F32)],
        ),
        out_shape=[
            jax.ShapeDtypeStruct((groups, rows, cols), BF16),
            jax.ShapeDtypeStruct((sources // PAIR, PAIR, cap), F32),
        ],
        compiler_params=pltpu.CompilerParams(vmem_limit_bytes=40 * 1024 * 1024),
    )(where, g, h, o)


def local(out_grad, routes, slots, combine_weight, saved_hidden, saved_out):
    nx, nz = lax.axis_size("x"), lax.axis_size("z")
    blocks = lax.axis_size("y") * lax.axis_size("c")
    cap, units = saved_hidden.shape[3:]
    cols = out_grad.shape[1]
    split = cols // saved_out.shape[4]
    experts = blocks // split
    topk = routes.shape[1]
    me = lax.axis_index("y") * lax.axis_size("c") + lax.axis_index("c")
    where = jnp.stack([me // split, me % split]).astype(jnp.int32)

    names = routes.T[None] == jnp.arange(experts, dtype=jnp.int32)[:, None, None]
    slot_of = jnp.sum(jnp.where(names, slots.T[None].astype(F32), 0.0), axis=1)
    weight_of = jnp.sum(jnp.where(names, combine_weight.T[None].astype(F32), 0.0), axis=1)
    meta = jnp.concatenate([slot_of, weight_of, jnp.zeros((META - 2 * experts, slot_of.shape[1]), F32)])
    sent = jnp.concatenate([out_grad.T, meta.astype(BF16)], axis=0)
    gathered = lax.all_gather(sent, ("y", "c"), axis=0)

    h = saved_hidden[0, 0].transpose(0, 2, 1)
    o = saved_out[0, 0].transpose(0, 2, 1)
    term, scores = compute(where, gathered, h, o, nx)

    by_x = lax.all_to_all(term, "x", split_axis=0, concat_axis=0, tiled=True)
    returned = lax.all_to_all(
        scores.reshape(blocks, 1, cap), ("y", "c"), split_axis=0, concat_axis=0, tiled=True
    )
    live = units // nx
    quarter = jnp.sum(by_x.astype(F32), axis=0)[:live].astype(BF16)
    share = live * cols // nz
    block = -(-share // 1024) * 1024
    flat = jnp.pad(quarter.reshape(nz, share), ((0, 0), (0, block - share)))
    by_z = lax.all_to_all(
        flat.reshape(nz, block // 128, 128), "z", split_axis=0, concat_axis=0, tiled=True
    )
    summed = jnp.sum(by_z.astype(F32), axis=0).astype(BF16)
    weight_grad = summed.reshape(1, block)[:, :share]

    combined = jnp.sum(returned.reshape(experts, split, cap), axis=1)
    router_grad = jnp.sum(jnp.where(names, combined[:, None, :], 0.0), axis=0).T
    return (weight_grad, router_grad)


def solution(mesh):
    nx = {64: 4, 4: 2}[mesh.shape["dp"]]
    grid = Mesh(
        mesh.devices.reshape(nx, mesh.shape["dp"] // nx, mesh.shape["expert"] // 2, 2),
        ("x", "z", "y", "c"),
    )
    rows = P(("x", "z", "y", "c"), None)
    saved = P(("x", "z"), ("y", "c"), None, None, None)
    return jax.shard_map(
        local,
        mesh=grid,
        in_specs=(rows, rows, rows, rows, saved, saved),
        out_specs=(P(("y", "c"), ("x", "z")), rows),
        check_vma=False,
    )
```

time: 500 us -> 159 us (0.32)
  the two profiles are of different devices: /device:TPU:8 before, /device:TPU:64 now
where the time goes in v1:
time: 159 us
  waiting for transfers between devices  83.3 us (52%)
  blocking collectives  21 us (13%)
  starting transfers between devices  17.6 us (11%)
  between operations  14.1 us (9%)
  local copies, waits for them, and re-layouts  11.2 us (7%)
  Pallas kernels  8.66 us (5%)
  other arithmetic  2.98 us (2%)
    all_gather x1, waiting for transfers between devices, local(): gathered = lax.all_gather(sent, ('y', 'c'), axis=0)  60.1 us
    all_to_all x1, blocking collectives, local(): by_x = lax.all_to_all(term, 'x', split_axis=0, concat_axis=0, tiled=True)  21 us
    all_to_all x1, waiting for transfers between devices, local(): lax.all_to_all(flat.reshape(nz, block // 128, 128), 'z', split_axis=0, co...  17.4 us
    all_to_all x1, starting transfers between devices, local(): lax.all_to_all(flat.reshape(nz, block // 128, 128), 'z', split_axis=0, co...  13.3 us
    pallas_call x1, Pallas kernels, compute(): pl.pallas_call(compute_kernel, grid_spec=pltpu.PrefetchScalarGridSpec(num...  8.66 us
    unnamed x11, local copies, waits for them, and re-layouts  6.85 us
    all_to_all x1, waiting for transfers between devices, local(): lax.all_to_all(scores.reshape(blocks, 1, cap), ('y', 'c'), split_axis=0,...  5.87 us
    all_to_all x1, starting transfers between devices, local(): lax.all_to_all(scores.reshape(blocks, 1, cap), ('y', 'c'), split_axis=0,...  4.29 us
  transfers between devices with their start and end apart: 3, of which 3 were waited for; matrix products, arithmetic and copies ran while one was open for 1% of the time, Pallas kernels for 0%

profile of v1, /device:TPU:64, one launch (start us, length us, event | category | flops | bytes accessed | tf_op | source)
XLA Modules:
  0.0 158.9 jit_solution(11834292777787362684)
XLA Ops:
  7.2 0.0 all-gather.3.cloned.1.call-start
  7.2 0.7 convert_bitcast_fusion.1
  7.9 0.7 convert_bitcast_fusion
  8.6 0.7 select_reduce_fusion
  9.3 3.8 %concatenate.6 = bf16[1456,128]{1,0:T(8,128)(2,1)} concatenate(bf16[1440,128]{1,0:T(8,128)(2,1)} %bitcast.35, bf16[4,128]{1,0:T(4,128)(2,1)S(1)} %get-tuple-element.7, bf16[4,128]{1,0:T(4,128)(2,1)S(1)} %get-tuple-element.6, bf16[8,128]{1,0:T(8,128)(2,1)S(1)} %broadcast_in_dim.39), dimensions={0} | concatenate | bytes 745472 | tf_op jit(solution)/shard_map/concatenate | solution.py:113
  13.1 0.0 all-gather.3.cloned.1.call-update
  13.1 0.1 pad_add_fusion.where_ref
  13.2 60.1 %all-gather.3.cloned.1.call-done = bf16[23296,128]{1,0:T(8,128)(2,1)} async-done(((bf16[1456,128]{1,0:T(8,128)(2,1)}), bf16[23296,128]{1,0:T(8,128)(2,1)}) %all-gather.3.cloned.1.call-update) | async-done | bytes 5963792 | tf_op jit(solution)/shard_map/all_gather | solution.py:114
  73.3 0.0 copy-start
  73.3 2.7 %copy-done = bf16[23296,128]{1,0:T(8,128)(2,1)S(1)} copy-done((bf16[23296,128]{1,0:T(8,128)(2,1)S(1)}, bf16[23296,128]{1,0:T(8,128)(2,1)}, u32[]{:S(2)}) %copy-start) | copy-done | bytes 5963800
  76.0 0.0 copy-start.1
  76.0 1.4 copy-done.1
  77.3 0.0 copy-start.2
  77.4 1.4 copy-done.2
  78.7 8.7 %shard_map.77 = (bf16[4,96,1440]{2,1,0:T(8,128)(2,1)S(1)}, f32[8,2,128]{2,1,0:T(2,128)}) custom-call(s32[2]{0:T(128)S(1)} %pad_add_fusion.where_ref, bf16[16,1456,128]{2,1,0:T(8,128)(2,1)S(1)} %bitcast.31, bf16[16,360,128]{2,1,0:T(8,128)(2,1)S(1)} %bitcast.32, bf16[16,360,128]{2,1,0:T(8,128)(2,1)S(1)} %bitcast.33), custom_call_target="tpu_custom_call" | custom-call | tf_op jit(solution)/shard_map/pallas_call | solution.py:74
  87.4 21.0 %all_to_all.15 = bf16[4,96,1440]{2,1,0:T(8,128)(2,1)S(1)} all-to-all(bf16[4,96,1440]{2,1,0:T(8,128)(2,1)S(1)} %get-tuple-element.4), channel_id=1, replica_groups=mesh['x'=4,'z'=16,'y'=8,'c'=2] {'x'}, dimensions={0} | all-to-all | bytes 2211840 | tf_op jit(solution)/shard_map/all_to_all | solution.py:120
  108.3 4.3 %all-to-all-start.2 = ((f32[16,1,128]{2,1,0:T(1,128)}), f32[16,1,128]{2,1,0:T(1,128)S(1)}, u32[]{:S(2)}, u32[]{:S(2)}) async-start(f32[16,1,128]{2,1,0:T(1,128)} %bitcast.12), calls=%async_computation.2 | async-start | bytes 16384 | tf_op jit(solution)/shard_map/all_to_all | solution.py:121
  112.6 0.0 copy-start.3
  112.6 0.2 reduce.1
  112.8 0.6 reshape.25
  113.5 0.7 copy.10
  114.3 5.9 %all-to-all-done.2 = f32[16,1,128]{2,1,0:T(1,128)S(1)} async-done(((f32[16,1,128]{2,1,0:T(1,128)}), f32[16,1,128]{2,1,0:T(1,128)S(1)}, u32[]{:S(2)}, u32[]{:S(2)}) %all-to-all-start.2) | async-done | bytes 8224 | tf_op jit(solution)/shard_map/all_to_all | solution.py:121
  120.1 13.3 %all-to-all-start.1 = ((bf16[16,64,128]{2,1,0:T(8,128)(2,1)}), bf16[16,64,128]{2,1,0:T(8,128)(2,1)S(1)}, u32[]{:S(2)}, u32[]{:S(2)}) async-start(bf16[16,64,128]{2,1,0:T(8,128)(2,1)} %bitcast.19), calls=%async_computation.1 | async-start | bytes 524288 | tf_op jit(solution)/shard_map/all_to_all | solution.py:129
  133.4 0.0 copy-done.3
  133.5 0.6 fusion.2
  134.1 17.4 %all-to-all-done.1 = bf16[16,64,128]{2,1,0:T(8,128)(2,1)S(1)} async-done(((bf16[16,64,128]{2,1,0:T(8,128)(2,1)}), bf16[16,64,128]{2,1,0:T(8,128)(2,1)S(1)}, u32[]{:S(2)}, u32[]{:S(2)}) %all-to-all-start.1) | async-done | bytes 262176 | tf_op jit(solution)/shard_map/all_to_all | solution.py:129
  151.4 0.6 copy.13
  (3 shorter events, 0.1 us)
Async XLA Ops:
  7.2 66.1 %all-gather.3.cloned.1.call-start = ((), (), s32[]{:S(2)}) async-start(), calls=%async_computation.3 | async-start | bytes 6336512 | tf_op jit(solution)/shard_map/all_gather | solution.py:114
  73.3 2.7 %copy-start = (bf16[23296,128]{1,0:T(8,128)(2,1)S(1)}, bf16[23296,128]{1,0:T(8,128)(2,1)}, u32[]{:S(2)}) copy-start(bf16[23296,128]{1,0:T(8,128)(2,1)} %all-gather.3.cloned.1.call-done) | copy-start | bytes 17891332
  76.0 1.4 copy-start.1
  77.3 1.4 copy-start.2
  108.3 11.8 %all-to-all-start.2 = ((f32[16,1,128]{2,1,0:T(1,128)}), f32[16,1,128]{2,1,0:T(1,128)S(1)}, u32[]{:S(2)}, u32[]{:S(2)}) async-start(f32[16,1,128]{2,1,0:T(1,128)} %bitcast.12), calls=%async_computation.2 | async-start | bytes 16384 | tf_op jit(solution)/shard_map/all_to_all | solution.py:121
  112.6 20.8 %copy-start.3 = (s32[128,4]{0,1:T(4,128)S(1)}, s32[128,4]{0,1:T(4,128)}, u32[]{:S(2)}) copy-start(s32[128,4]{0,1:T(4,128)} %param.7) | copy-start | bytes 6148
  120.1 31.3 %all-to-all-start.1 = ((bf16[16,64,128]{2,1,0:T(8,128)(2,1)}), bf16[16,64,128]{2,1,0:T(8,128)(2,1)S(1)}, u32[]{:S(2)}, u32[]{:S(2)}) async-start(bf16[16,64,128]{2,1,0:T(8,128)(2,1)} %bitcast.19), calls=%async_computation.1 | async-start | bytes 524288 | tf_op jit(solution)/shard_map/all_to_all | solution.py:129
Sparse Core Ops, SparseCore 0:
  13.2 60.0 all-gather.2

commit v2 on v1

v2 whole, which is shorter than its diff:
```python
import jax
import jax.numpy as jnp
from jax import lax
from jax.experimental import pallas as pl
from jax.experimental.pallas import tpu as pltpu
from jax.sharding import Mesh, PartitionSpec as P

F32 = jnp.float32
BF16 = jnp.bfloat16
STEP = 4
SHIFT = 8
SPREAD = 16
VMEM = 56 * 1024 * 1024


def place_kernel(part_ref, meta_ref, h_ref, o_ref, hp_ref, op_ref):
    odd = lax.rem(part_ref[0], 2)
    cap = h_ref.shape[2]
    live, rows = h_ref.shape[1] // NX[0], hp_ref.shape[0] // NX[0]
    slot_row = lax.broadcasted_iota(jnp.int32, (cap, cap), 0)
    gap = jnp.zeros((SHIFT, cap), F32)
    blank = jnp.zeros((rows - live, cap), F32)
    for u in range(STEP):
        slot = meta_ref[u, 0:1, :].astype(jnp.int32)
        place = (slot_row == slot).astype(BF16)
        hidden = jnp.dot(h_ref[u], place, preferred_element_type=F32)
        out = jnp.dot(o_ref[u], place, preferred_element_type=F32)
        op_ref[u] = jnp.where(
            odd == 1, jnp.concatenate([gap, out], axis=0), jnp.concatenate([out, gap], axis=0)
        ).astype(BF16)
        spread = []
        for q in range(NX[0]):
            spread += [hidden[q * live : (q + 1) * live], blank]
        hp_ref[:, u * cap : (u + 1) * cap] = jnp.concatenate(spread, axis=0).astype(BF16)


def term_kernel(part_ref, meta_ref, g_ref, hp_ref, op_ref, w_ref, s_ref, acc):
    step = pl.program_id(0)
    part = part_ref[0]
    width = op_ref.shape[1]
    start = pl.multiple_of(part * (width - SHIFT) - SHIFT * lax.rem(part, 2), 16)
    groups, rows, _ = w_ref.shape
    rhs = []
    for u in range(STEP):
        weight = meta_ref[u, 1:2, :]
        window = g_ref[u, pl.ds(start, width), :].astype(F32)
        score = jnp.sum(op_ref[u].astype(F32) * window, axis=0, keepdims=True)
        s_ref[u] = jnp.broadcast_to(score, s_ref.shape[1:])
        rhs.append((g_ref[u].astype(F32) * weight).astype(BF16))
    term = lax.dot_general(
        hp_ref[...],
        jnp.concatenate(rhs, axis=1),
        (((1,), (1,)), ((), ())),
        preferred_element_type=F32,
    )

    @pl.when(step == 0)
    def _():
        acc[...] = term

    @pl.when(step > 0)
    def _():
        acc[...] += term

    @pl.when(step == pl.num_programs(0) - 1)
    def _():
        for q in range(groups):
            w_ref[q] = acc[q * rows : (q + 1) * rows, :].astype(BF16)


NX = [4]


def place(part, meta, h, o, rows):
    sources, units, cap = h.shape
    width = o.shape[1] + SHIFT
    return pl.pallas_call(
        place_kernel,
        grid_spec=pltpu.PrefetchScalarGridSpec(
            num_scalar_prefetch=1,
            grid=(sources // STEP,),
            in_specs=[
                pl.BlockSpec((STEP, 2, cap), lambda i, p: (i, 0, 0)),
                pl.BlockSpec((STEP, units, cap), lambda i, p: (i, 0, 0)),
                pl.BlockSpec((STEP, o.shape[1], cap), lambda i, p: (i, 0, 0)),
            ],
            out_specs=[
                pl.BlockSpec((NX[0] * rows, STEP * cap), lambda i, p: (0, i)),
                pl.BlockSpec((STEP, width, cap), lambda i, p: (i, 0, 0)),
            ],
        ),
        out_shape=[
            jax.ShapeDtypeStruct((NX[0] * rows, sources * cap), BF16),
            jax.ShapeDtypeStruct((sources, width, cap), BF16),
        ],
        compiler_params=pltpu.CompilerParams(vmem_limit_bytes=VMEM),
        cost_estimate=pl.CostEstimate(
            flops=4 * sources * units * cap * cap, bytes_accessed=8 * sources * units * cap, transcendentals=0
        ),
    )(part, meta, h, o)


def weight_term(part, meta, g, hp, op, rows):
    sources, cols, cap = g.shape
    width = op.shape[1]
    return pl.pallas_call(
        term_kernel,
        grid_spec=pltpu.PrefetchScalarGridSpec(
            num_scalar_prefetch=1,
            grid=(sources // STEP,),
            in_specs=[
                pl.BlockSpec((STEP, 2, cap), lambda i, p: (i, 0, 0)),
                pl.BlockSpec((STEP, cols, cap), lambda i, p: (i, 0, 0)),
                pl.BlockSpec((NX[0] * rows, STEP * cap), lambda i, p: (0, i)),
                pl.BlockSpec((STEP, width, cap), lambda i, p: (i, 0, 0)),
            ],
            out_specs=[
                pl.BlockSpec((NX[0], rows, cols), lambda i, p: (0, 0, 0)),
                pl.BlockSpec((STEP, SPREAD, cap), lambda i, p: (i, 0, 0)),
            ],
            scratch_shapes=[pltpu.VMEM((NX[0] * rows, cols), F32)],
        ),
        out_shape=[
            jax.ShapeDtypeStruct((NX[0], rows, cols), BF16),
            jax.ShapeDtypeStruct((sources, SPREAD, cap), F32),
        ],
        compiler_params=pltpu.CompilerParams(vmem_limit_bytes=VMEM),
        cost_estimate=pl.CostEstimate(
            flops=2 * sources * cap * NX[0] * rows * cols, bytes_accessed=2 * sources * cols * cap, transcendentals=0
        ),
    )(part, meta, g, hp, op)


def local(out_grad, routes, slots, combine_weight, saved_hidden, saved_out):
    nx, nz = lax.axis_size("x"), lax.axis_size("z")
    NX[0] = nx
    blocks = lax.axis_size("y") * lax.axis_size("c")
    cap, units = saved_hidden.shape[3:]
    cols = out_grad.shape[1]
    split = cols // saved_out.shape[4]
    experts = blocks // split
    me = lax.axis_index("y") * lax.axis_size("c") + lax.axis_index("c")
    part = (me % split).reshape(1).astype(jnp.int32)
    live = units // nx
    rows = -(-live // 16) * 16

    gathered = lax.all_gather(out_grad.T, ("y", "c"), axis=0)

    names = routes.T[None] == jnp.arange(experts, dtype=jnp.int32)[:, None, None]
    slot_of = jnp.sum(jnp.where(names, slots.T[None].astype(F32), 0.0), axis=1)
    weight_of = jnp.sum(jnp.where(names, combine_weight.T[None].astype(F32), 0.0), axis=1)
    sent = jnp.repeat(jnp.stack([slot_of, weight_of], axis=1), split, axis=0)
    meta = lax.all_to_all(sent, ("y", "c"), split_axis=0, concat_axis=0, tiled=True)

    h = saved_hidden[0, 0].transpose(0, 2, 1)
    o = saved_out[0, 0].transpose(0, 2, 1)
    hp, op = place(part, meta, h, o, rows)
    term, scores = weight_term(part, meta, gathered, hp, op, rows)

    everyones = lax.all_gather(scores, ("y", "c"), axis=0)
    by_x = lax.all_to_all(term, "x", split_axis=0, concat_axis=0, tiled=True)
    quarter = jnp.sum(by_x.astype(F32), axis=0)[:live].astype(BF16)
    share = live * cols // nz
    block = -(-share // 1024) * 1024
    flat = jnp.pad(quarter.reshape(nz, share), ((0, 0), (0, block - share)))
    by_z = lax.all_to_all(
        flat.reshape(nz, block // 128, 128), "z", split_axis=0, concat_axis=0, tiled=True
    )
    summed = jnp.sum(by_z.astype(F32), axis=0).astype(BF16)
    weight_grad = summed.reshape(1, block)[:, :share]

    returned = lax.dynamic_slice_in_dim(everyones, me, 1, axis=1)[:, 0, 0]
    combined = jnp.sum(returned.reshape(experts, split, cap), axis=1)
    router_grad = jnp.sum(jnp.where(names, combined[:, None, :], 0.0), axis=0).T
    return (weight_grad, router_grad)


def solution(mesh):
    nx = {64: 4, 4: 2}[mesh.shape["dp"]]
    grid = Mesh(
        mesh.devices.reshape(nx, mesh.shape["dp"] // nx, mesh.shape["expert"] // 2, 2),
        ("x", "z", "y", "c"),
    )
    rows = P(("x", "z", "y", "c"), None)
    saved = P(("x", "z"), ("y", "c"), None, None, None)
    return jax.shard_map(
        local,
        mesh=grid,
        in_specs=(rows, rows, rows, rows, saved, saved),
        out_specs=(P(("y", "c"), ("x", "z")), rows),
        check_vma=False,
    )
```

time: 159 us -> 142 us (0.89)
  the two profiles are of different devices: /device:TPU:64 before, /device:TPU:8 now
where the time goes in v2:
time: 142 us
  waiting for transfers between devices  56.7 us (40%)
  starting transfers between devices  29.5 us (21%)
  blocking collectives  21.2 us (15%)
  between operations  14.1 us (10%)
  Pallas kernels  13 us (9%)
  local copies, waits for them, and re-layouts  4.14 us (3%)
  other arithmetic  2.9 us (2%)
    all_gather x1, waiting for transfers between devices, local(): gathered = lax.all_gather(out_grad.T, ('y', 'c'), axis=0)  31.9 us
    all_to_all x1, blocking collectives, local(): by_x = lax.all_to_all(term, 'x', split_axis=0, concat_axis=0, tiled=True)  21.2 us
    all_to_all x1, waiting for transfers between devices, local(): lax.all_to_all(flat.reshape(nz, block // 128, 128), 'z', split_axis=0, co...  17.9 us
    all_to_all x1, starting transfers between devices, local(): lax.all_to_all(sent, ('y', 'c'), split_axis=0, concat_axis=0, tiled=True)  16.4 us
    all_to_all x1, starting transfers between devices, local(): lax.all_to_all(flat.reshape(nz, block // 128, 128), 'z', split_axis=0, co...  13 us
    pallas_call x1, Pallas kernels, weight_term(): pl.pallas_call(term_kernel, grid_spec=pltpu.PrefetchScalarGridSpec(num_sc...  7.81 us
    all_to_all x1, waiting for transfers between devices, local(): lax.all_to_all(sent, ('y', 'c'), split_axis=0, concat_axis=0, tiled=True)  6.22 us
    pallas_call x1, Pallas kernels, place(): pl.pallas_call(place_kernel, grid_spec=pltpu.PrefetchScalarGridSpec(num_s...  5.21 us
  transfers between devices with their start and end apart: 4, of which 3 were waited for; matrix products, arithmetic and copies ran while one was open for 4% of the time, Pallas kernels for 4%

profile of v2, /device:TPU:8, one launch (start us, length us, event | category | flops | bytes accessed | tf_op | source)
XLA Modules:
  0.0 141.5 jit_solution(9625411877366078045)
XLA Ops:
  7.2 0.0 all-gather.5.cloned.1.call-start
  7.2 0.7 all-gather.5.cloned.1.call-update
  7.9 0.7 convert_bitcast_fusion
  8.6 0.7 convert_bitcast_fusion.1
  9.3 0.7 select_reduce_fusion.1
  10.0 0.6 broadcast_in_dim.39
  10.6 16.4 %all-to-all-start = ((f32[16,2,128]{2,1,0:T(2,128)}), f32[16,2,128]{2,1,0:T(2,128)S(1)}, u32[]{:S(2)}, u32[]{:S(2)}) async-start(f32[16,2,128]{2,1,0:T(2,128)} %bitcast.6), calls=%async_computation | async-start | bytes 32768 | tf_op jit(solution)/shard_map/all_to_all | solution.py:153
  27.0 0.0 all-gather.7.cloned.1.call-start
  27.0 6.2 %all-to-all-done.meta_ref = f32[16,2,128]{2,1,0:T(2,128)S(1)} async-done(((f32[16,2,128]{2,1,0:T(2,128)}), f32[16,2,128]{2,1,0:T(2,128)S(1)}, u32[]{:S(2)}, u32[]{:S(2)}) %all-to-all-start) | async-done | bytes 16416 | tf_op jit(solution)/shard_map/all_to_all | solution.py:153
  33.3 0.0 copy-start
  33.3 0.6 copy-done
  33.9 5.2 %shard_map.77 = (bf16[384,2048]{1,0:T(8,128)(2,1)}, bf16[16,368,128]{2,1,0:T(8,128)(2,1)}) custom-call(s32[1]{0:T(128)} %bitcast.part_ref, f32[16,2,128]{2,1,0:T(2,128)} %copy-done, bf16[16,360,128]{2,1,0:T(8,128)(2,1)} %bitcast.32, bf16[16,360,128]{2,1,0:T(8,128)(2,1)} %bitcast.33), custom_call_target="tpu_custom_call" | custom-call | flops 377487360 | bytes 5898240 | tf_op jit(solution)/shard_map/pallas_call | solution.py:77
  39.1 31.9 %all-gather.5.cloned.1.call-done = bf16[23040,128]{1,0:T(8,128)(2,1)} async-done(((bf16[1440,128]{1,0:T(8,128)(2,1)}), bf16[23040,128]{1,0:T(8,128)(2,1)}) %all-gather.5.cloned.1.call-update) | async-done | bytes 5898256 | tf_op jit(solution)/shard_map/all_gather | solution.py:147
  71.0 7.8 %shard_map.78 = (bf16[4,96,1440]{2,1,0:T(8,128)(2,1)}, f32[16,16,128]{2,1,0:T(8,128)}) custom-call(s32[1]{0:T(128)} %bitcast.part_ref, f32[16,2,128]{2,1,0:T(2,128)} %copy-done, bf16[16,1440,128]{2,1,0:T(8,128)(2,1)} %bitcast.31, bf16[384,2048]{1,0:T(8,128)(2,1)} %get-tuple-element.6.hp_ref, bf16[16,368,128]{2,1,0:T(8,128)(2,1)} %get-tuple-element.7.op_ref), custom_call_target="tpu_custom_call" | custom-call | flops 2264924160 | bytes 5898240 | tf_op jit(solution)/shard_map/pallas_call | solution.py:106
  78.8 0.0 all-gather.7.cloned.1.call-update
  78.9 21.2 %all_to_all.15 = bf16[4,96,1440]{2,1,0:T(8,128)(2,1)S(1)} all-to-all(bf16[4,96,1440]{2,1,0:T(8,128)(2,1)} %get-tuple-element.8), channel_id=1, replica_groups=mesh['x'=4,'z'=16,'y'=8,'c'=2] {'x'}, dimensions={0} | all-to-all | bytes 2211840 | tf_op jit(solution)/shard_map/all_to_all | solution.py:161
  100.0 0.2 reduce.1
  100.2 0.0 copy-start.1
  100.2 0.6 reshape.27
  100.9 0.8 copy.9
  101.7 13.0 %all-to-all-start.2 = ((bf16[16,64,128]{2,1,0:T(8,128)(2,1)}), bf16[16,64,128]{2,1,0:T(8,128)(2,1)S(1)}, u32[]{:S(2)}, u32[]{:S(2)}) async-start(bf16[16,64,128]{2,1,0:T(8,128)(2,1)} %bitcast.19), calls=%async_computation.2 | async-start | bytes 524288 | tf_op jit(solution)/shard_map/all_to_all | solution.py:166
  114.7 17.9 %all-to-all-done.2 = bf16[16,64,128]{2,1,0:T(8,128)(2,1)S(1)} async-done(((bf16[16,64,128]{2,1,0:T(8,128)(2,1)}), bf16[16,64,128]{2,1,0:T(8,128)(2,1)S(1)}, u32[]{:S(2)}, u32[]{:S(2)}) %all-to-all-start.2) | async-done | bytes 262176 | tf_op jit(solution)/shard_map/all_to_all | solution.py:166
  132.6 0.6 copy.12
  133.2 0.0 all-gather.7.cloned.1.call-done
  133.2 0.8 constant_dynamic-slice_fusion
  134.1 0.0 copy-done.1
  134.1 0.6 fusion.2
  (4 shorter events, 0.1 us)
Async XLA Ops:
  7.2 63.9 %all-gather.5.cloned.1.call-start = ((), (), s32[]{:S(2)}) async-start(), calls=%async_computation.3 | async-start | bytes 6266880 | tf_op jit(solution)/shard_map/all_gather | solution.py:147
  10.6 22.7 %all-to-all-start = ((f32[16,2,128]{2,1,0:T(2,128)}), f32[16,2,128]{2,1,0:T(2,128)S(1)}, u32[]{:S(2)}, u32[]{:S(2)}) async-start(f32[16,2,128]{2,1,0:T(2,128)} %bitcast.6), calls=%async_computation | async-start | bytes 32768 | tf_op jit(solution)/shard_map/all_to_all | solution.py:153
  27.0 106.3 %all-gather.7.cloned.1.call-start = ((), (), s32[]{:S(2)}) async-start(), calls=%async_computation.4 | async-start | bytes 2228224 | tf_op jit(solution)/shard_map/all_gather | solution.py:160
  33.3 0.6 copy-start
  100.2 33.9 %copy-start.1 = (s32[128,4]{0,1:T(4,128)S(1)}, s32[128,4]{0,1:T(4,128)}, u32[]{:S(2)}) copy-start(s32[128,4]{0,1:T(4,128)} %param.7) | copy-start | bytes 6148
  101.7 30.9 %all-to-all-start.2 = ((bf16[16,64,128]{2,1,0:T(8,128)(2,1)}), bf16[16,64,128]{2,1,0:T(8,128)(2,1)S(1)}, u32[]{:S(2)}, u32[]{:S(2)}) async-start(bf16[16,64,128]{2,1,0:T(8,128)(2,1)} %bitcast.19), calls=%async_computation.2 | async-start | bytes 524288 | tf_op jit(solution)/shard_map/all_to_all | solution.py:166
Sparse Core Ops, SparseCore 0:
  10.7 60.2 all-gather.4
  79.0 46.9 all-gather.6

commit v3 on v2

v3 whole, which is shorter than its diff:
```python
import functools

import jax
import jax.numpy as jnp
from jax import lax
from jax.experimental import pallas as pl
from jax.experimental.pallas import tpu as pltpu
from jax.sharding import Mesh, PartitionSpec as P

F32 = jnp.float32
BF16 = jnp.bfloat16
STEP = 4
SHIFT = 8
SPREAD = 16
FOLD = 4
LANE = 128
TILE = 256
VMEM = 56 * 1024 * 1024


def place_kernel(part_ref, meta_ref, h_ref, o_ref, hp_ref, op_ref, tall):
    odd = lax.rem(part_ref[0], 2)
    units, cap = h_ref.shape[1:]
    rows = hp_ref.shape[0] // FOLD
    slot_row = lax.broadcasted_iota(jnp.int32, (cap, cap), 0)
    gap = jnp.zeros((SHIFT, cap), F32)
    blank = jnp.zeros((rows - units // FOLD, cap), F32)
    for u in range(STEP):
        slot = meta_ref[u, 0:1, :].astype(jnp.int32)
        place = (slot_row == slot).astype(BF16)
        tall[...] = jnp.dot(h_ref[u], place, preferred_element_type=F32)
        out = jnp.dot(o_ref[u], place, preferred_element_type=F32)
        op_ref[u] = jnp.where(
            odd == 1, jnp.concatenate([gap, out], axis=0), jnp.concatenate([out, gap], axis=0)
        ).astype(BF16)
        for m in range(FOLD):
            picked = tall[pl.ds(m, units // FOLD, stride=FOLD), :]
            hp_ref[m * rows : (m + 1) * rows, u * cap : (u + 1) * cap] = jnp.concatenate(
                [picked, blank], axis=0
            ).astype(BF16)


def term_kernel(shape, part_ref, meta_ref, g_ref, hp_ref, op_ref, w_ref, s_ref, acc, rhs, flat):
    units, nx, nh, nl = shape
    step = pl.program_id(0)
    part = part_ref[0]
    width = op_ref.shape[1]
    cols, cap = g_ref.shape[1:]
    wide = rhs.shape[0]
    start = pl.multiple_of(part * (width - SHIFT) - SHIFT * lax.rem(part, 2), 16)

    @pl.when(step == 0)
    def _():
        rhs[cols:, :] = jnp.zeros((wide - cols, STEP * cap), BF16)

    for u in range(STEP):
        weight = meta_ref[u, 1:2, :]
        window = g_ref[u, pl.ds(start, width), :].astype(F32)
        score = jnp.sum(op_ref[u].astype(F32) * window, axis=0, keepdims=True)
        s_ref[u] = jnp.broadcast_to(score, s_ref.shape[1:])
        rhs[:cols, u * cap : (u + 1) * cap] = (g_ref[u].astype(F32) * weight).astype(BF16)

    def add(first):
        for n in range(0, wide, TILE):
            term = lax.dot_general(
                hp_ref[...],
                rhs[n : n + TILE, :],
                (((1,), (1,)), ((), ())),
                preferred_element_type=F32,
            )
            acc[:, n : n + TILE] = term if first else acc[:, n : n + TILE] + term

    pl.when(step == 0)(lambda: add(True))
    pl.when(step > 0)(lambda: add(False))

    @pl.when(step == pl.num_programs(0) - 1)
    def _():
        live, rows = units // FOLD, acc.shape[0] // FOLD
        span = FOLD * cols // LANE
        whole = units * cols // LANE
        flat[whole:, :] = jnp.zeros((flat.shape[0] - whole, LANE), F32)
        tail = None
        for m in range(FOLD):
            lead, offset = divmod(m * cols, LANE)
            lines = acc[m * rows : (m + 1) * rows, :]
            lines = pltpu.roll(lines, offset, 1) if offset else lines
            for t in range(wide // LANE):
                piece = lines[:live, t * LANE : (t + 1) * LANE]
                if t == 0 and offset:
                    piece = piece + tail
                tail = piece
                end = (lead + t + 1) * LANE
                if end <= (m + 1) * cols:
                    flat[pl.ds(lead + t, live, stride=span), :] = piece
                elif end - LANE < (m + 1) * cols:
                    break
        size = w_ref.shape[1] // nh
        share = units * cols // (nx * nh * nl)
        lane = lax.broadcasted_iota(jnp.int32, (size, LANE), 1)
        for q in range(nx * nh * nl):
            x, z = divmod(q, nh * nl)
            base, offset = divmod(q * share, LANE)
            own = flat[base : base + size, :]
            if offset:
                after = flat[base + 1 : base + 1 + size, :]
                own = pltpu.roll(jnp.where(lane < offset, after, own), LANE - offset, 1)
            h, l = divmod(z, nl)
            w_ref[x * nl + l, h * size : (h + 1) * size, :] = own.astype(BF16)


def place(part, meta, h, o, rows):
    sources, units, cap = h.shape
    width = o.shape[1] + SHIFT
    return pl.pallas_call(
        place_kernel,
        grid_spec=pltpu.PrefetchScalarGridSpec(
            num_scalar_prefetch=1,
            grid=(sources // STEP,),
            in_specs=[
                pl.BlockSpec((STEP, 2, cap), lambda i, p: (i, 0, 0)),
                pl.BlockSpec((STEP, units, cap), lambda i, p: (i, 0, 0)),
                pl.BlockSpec((STEP, o.shape[1], cap), lambda i, p: (i, 0, 0)),
            ],
            out_specs=[
                pl.BlockSpec((FOLD * rows, STEP * cap), lambda i, p: (0, i)),
                pl.BlockSpec((STEP, width, cap), lambda i, p: (i, 0, 0)),
            ],
            scratch_shapes=[pltpu.VMEM((units, cap), F32)],
        ),
        out_shape=[
            jax.ShapeDtypeStruct((FOLD * rows, sources * cap), BF16),
            jax.ShapeDtypeStruct((sources, width, cap), BF16),
        ],
        compiler_params=pltpu.CompilerParams(vmem_limit_bytes=VMEM),
        cost_estimate=pl.CostEstimate(
            flops=4 * sources * units * cap * cap, bytes_accessed=8 * sources * units * cap, transcendentals=0
        ),
    )(part, meta, h, o)


def weight_term(part, meta, g, hp, op, shape):
    units, nx, nh, nl = shape
    sources, cols, cap = g.shape
    width = op.shape[1]
    high = hp.shape[0]
    wide = -(-cols // TILE) * TILE
    share = units * cols // (nx * nh * nl)
    size = -(-share // (16 * LANE)) * 16
    lines = -(-((nx * nh * nl - 1) * share // LANE + size + 1) // 8) * 8
    return pl.pallas_call(
        functools.partial(term_kernel, shape),
        grid_spec=pltpu.PrefetchScalarGridSpec(
            num_scalar_prefetch=1,
            grid=(sources // STEP,),
            in_specs=[
                pl.BlockSpec((STEP, 2, cap), lambda i, p: (i, 0, 0)),
                pl.BlockSpec((STEP, cols, cap), lambda i, p: (i, 0, 0)),
                pl.BlockSpec((high, STEP * cap), lambda i, p: (0, i)),
                pl.BlockSpec((STEP, width, cap), lambda i, p: (i, 0, 0)),
            ],
            out_specs=[
                pl.BlockSpec((nx * nl, nh * size, LANE), lambda i, p: (0, 0, 0)),
                pl.BlockSpec((STEP, SPREAD, cap), lambda i, p: (i, 0, 0)),
            ],
            scratch_shapes=[
                pltpu.VMEM((high, wide), F32),
                pltpu.VMEM((wide, STEP * cap), BF16),
                pltpu.VMEM((lines, LANE), F32),
            ],
        ),
        out_shape=[
            jax.ShapeDtypeStruct((nx * nl, nh * size, LANE), BF16),
            jax.ShapeDtypeStruct((sources, SPREAD, cap), F32),
        ],
        compiler_params=pltpu.CompilerParams(vmem_limit_bytes=VMEM),
        cost_estimate=pl.CostEstimate(
            flops=2 * sources * cap * high * wide, bytes_accessed=2 * sources * cols * cap, transcendentals=0
        ),
    )(part, meta, g, hp, op)


def local(out_grad, routes, slots, combine_weight, saved_hidden, saved_out):
    nx, nh, nl = (lax.axis_size(name) for name in ("x", "zh", "zl"))
    blocks = lax.axis_size("y") * lax.axis_size("c")
    cap, units = saved_hidden.shape[3:]
    cols = out_grad.shape[1]
    split = cols // saved_out.shape[4]
    experts = blocks // split
    me = lax.axis_index("y") * lax.axis_size("c") + lax.axis_index("c")
    part = (me % split).reshape(1).astype(jnp.int32)
    rows = -(-(units // FOLD) // 16) * 16

    gathered = lax.all_gather(out_grad.T, ("y", "c"), axis=0)

    names = routes.T[None] == jnp.arange(experts, dtype=jnp.int32)[:, None, None]
    slot_of = jnp.sum(jnp.where(names, slots.T[None].astype(F32), 0.0), axis=1)
    weight_of = jnp.sum(jnp.where(names, combine_weight.T[None].astype(F32), 0.0), axis=1)
    sent = jnp.repeat(jnp.stack([slot_of, weight_of], axis=1), split, axis=0)
    meta = lax.all_to_all(sent, ("y", "c"), split_axis=0, concat_axis=0, tiled=True)

    h = saved_hidden[0, 0].transpose(0, 2, 1)
    o = saved_out[0, 0].transpose(0, 2, 1)
    hp, op = place(part, meta, h, o, rows)
    term, scores = weight_term(part, meta, gathered, hp, op, (units, nx, nh, nl))

    everyones = lax.all_gather(scores, ("y", "c"), axis=0)
    first = lax.all_to_all(term, ("x", "zl"), split_axis=0, concat_axis=0, tiled=True)
    partial_sum = jnp.sum(first.astype(F32), axis=0).astype(BF16)
    second = lax.all_to_all(
        partial_sum.reshape(nh, -1, LANE), "zh", split_axis=0, concat_axis=0, tiled=True
    )
    summed = jnp.sum(second.astype(F32), axis=0).astype(BF16)
    weight_grad = summed.reshape(1, -1)[:, : units * cols // (nx * nh * nl)]

    returned = lax.dynamic_slice_in_dim(everyones, me, 1, axis=1)[:, 0, 0]
    combined = jnp.sum(returned.reshape(experts, split, cap), axis=1)
    router_grad = jnp.sum(jnp.where(names, combined[:, None, :], 0.0), axis=0).T
    return (weight_grad, router_grad)


def solution(mesh):
    nx = {64: 4, 4: 2}[mesh.shape["dp"]]
    grid = Mesh(
        mesh.devices.reshape(nx, mesh.shape["dp"] // nx // 2, 2, mesh.shape["expert"] // 2, 2),
        ("x", "zh", "zl", "y", "c"),
    )
    rows = P(("x", "zh", "zl", "y", "c"), None)
    saved = P(("x", "zh", "zl"), ("y", "c"), None, None, None)
    return jax.shard_map(
        local,
        mesh=grid,
        in_specs=(rows, rows, rows, rows, saved, saved),
        out_specs=(P(("y", "c"), ("x", "zh", "zl")), rows),
        check_vma=False,
    )
```

time: 142 us -> 137 us (0.965)
  waiting for transfers between devices: 56.7 us -> 52.5 us
  local copies, waits for them, and re-layouts: 4.14 us -> 2.71 us
    all_to_all x1, waiting for transfers between devices: 17.9 us -> 1.02 us  [local(): lax.all_to_all(partial_sum.reshape(nh, -1, LANE), 'zh', split_axis=0, con...]
    all_gather x1, waiting for transfers between devices: 0.01 us -> 12.8 us  [local(): everyones = lax.all_gather(scores, ('y', 'c'), axis=0)]
  transfers between devices with their start and end apart: 4 -> 4, of which waited for: 3 -> 4; matrix products, arithmetic and copies ran while one was open for 4% -> 4% of each run, Pallas kernels for 4% -> 4%
where the time goes in v3:
time: 137 us
  waiting for transfers between devices  52.5 us (38%)
  starting transfers between devices  28.6 us (21%)
  blocking collectives  21.3 us (16%)
  Pallas kernels  14.2 us (10%)
  between operations  14.1 us (10%)
  other arithmetic  3.5 us (3%)
  local copies, waits for them, and re-layouts  2.71 us (2%)
    all_gather x1, waiting for transfers between devices, local(): gathered = lax.all_gather(out_grad.T, ('y', 'c'), axis=0)  31.8 us
    all_to_all x1, blocking collectives, local(): lax.all_to_all(term, ('x', 'zl'), split_axis=0, concat_axis=0, tiled=True)  21.3 us
    all_to_all x1, starting transfers between devices, local(): lax.all_to_all(sent, ('y', 'c'), split_axis=0, concat_axis=0, tiled=True)  16.4 us
    all_gather x1, waiting for transfers between devices, local(): everyones = lax.all_gather(scores, ('y', 'c'), axis=0)  12.8 us
    all_to_all x1, starting transfers between devices, local(): lax.all_to_all(partial_sum.reshape(nh, -1, LANE), 'zh', split_axis=0, con...  12.1 us
    pallas_call x1, Pallas kernels, weight_term(): pl.pallas_call(functools.partial(term_kernel, shape), grid_spec=pltpu.Pre...  8.82 us
    all_to_all x1, waiting for transfers between devices, local(): lax.all_to_all(sent, ('y', 'c'), split_axis=0, concat_axis=0, tiled=True)  6.22 us
    pallas_call x1, Pallas kernels, place(): pl.pallas_call(place_kernel, grid_spec=pltpu.PrefetchScalarGridSpec(num_s...  5.33 us
  transfers between devices with their start and end apart: 4, of which 4 were waited for; matrix products, arithmetic and copies ran while one was open for 4% of the time, Pallas kernels for 4%

profile of v3, /device:TPU:8, one launch (start us, length us, event | category | flops | bytes accessed | tf_op | source)
XLA Modules:
  0.0 136.9 jit_solution(5356241429994176402)
XLA Ops:
  7.2 0.0 all-gather.5.cloned.1.call-start
  7.2 0.7 all-gather.5.cloned.1.call-update
  7.9 0.7 convert_bitcast_fusion
  8.6 0.7 convert_bitcast_fusion.1
  9.3 0.7 select_reduce_fusion.1
  10.0 0.6 broadcast_in_dim.39
  10.6 16.4 %all-to-all-start = ((f32[16,2,128]{2,1,0:T(2,128)}), f32[16,2,128]{2,1,0:T(2,128)S(1)}, u32[]{:S(2)}, u32[]{:S(2)}) async-start(f32[16,2,128]{2,1,0:T(2,128)} %bitcast.6), calls=%async_computation | async-start | bytes 32768 | tf_op jit(solution)/shard_map/all_to_all | solution.py:199
  27.0 0.0 all-gather.7.cloned.1.call-start
  27.0 6.2 %all-to-all-done.meta_ref = f32[16,2,128]{2,1,0:T(2,128)S(1)} async-done(((f32[16,2,128]{2,1,0:T(2,128)}), f32[16,2,128]{2,1,0:T(2,128)S(1)}, u32[]{:S(2)}, u32[]{:S(2)}) %all-to-all-start) | async-done | bytes 16416 | tf_op jit(solution)/shard_map/all_to_all | solution.py:199
  33.3 0.0 copy-start
  33.3 0.6 copy-done
  33.9 5.3 %shard_map.77 = (bf16[384,2048]{1,0:T(8,128)(2,1)}, bf16[16,368,128]{2,1,0:T(8,128)(2,1)}) custom-call(s32[1]{0:T(128)} %bitcast.part_ref, f32[16,2,128]{2,1,0:T(2,128)} %copy-done, bf16[16,360,128]{2,1,0:T(8,128)(2,1)} %bitcast.29, bf16[16,360,128]{2,1,0:T(8,128)(2,1)} %bitcast.30), custom_call_target="tpu_custom_call" | custom-call | flops 377487360 | bytes 5898240 | tf_op jit(solution)/shard_map/pallas_call | solution.py:114
  39.2 31.8 %all-gather.5.cloned.1.call-done = bf16[23040,128]{1,0:T(8,128)(2,1)} async-done(((bf16[1440,128]{1,0:T(8,128)(2,1)}), bf16[23040,128]{1,0:T(8,128)(2,1)}) %all-gather.5.cloned.1.call-update) | async-done | bytes 5898256 | tf_op jit(solution)/shard_map/all_gather | solution.py:193
  71.0 8.8 %shard_map.78 = (bf16[8,512,128]{2,1,0:T(8,128)(2,1)}, f32[16,16,128]{2,1,0:T(8,128)}) custom-call(s32[1]{0:T(128)} %bitcast.part_ref, f32[16,2,128]{2,1,0:T(2,128)} %copy-done, bf16[16,1440,128]{2,1,0:T(8,128)(2,1)} %bitcast.28, bf16[384,2048]{1,0:T(8,128)(2,1)} %get-tuple-element.6.hp_ref, bf16[16,368,128]{2,1,0:T(8,128)(2,1)} %get-tuple-element.7.op_ref), custom_call_target="tpu_custom_call" | custom-call | flops 2415919104 | bytes 5898240 | tf_op jit(solution)/shard_map/pallas_call | solution.py:150
  79.8 0.0 all-gather.7.cloned.1.call-update
  79.9 0.0 copy-start.1
  79.9 21.3 %all_to_all.15 = bf16[8,512,128]{2,1,0:T(8,128)(2,1)S(1)} all-to-all(bf16[8,512,128]{2,1,0:T(8,128)(2,1)} %get-tuple-element.8), channel_id=1, replica_groups=mesh['x'=4,'zh'=8,'zl'=2,'y'=8,'c'=2] {'x','zl'}, dimensions={0} | all-to-all | bytes 2097152 | tf_op jit(solution)/shard_map/all_to_all | solution.py:207
  101.2 0.8 reduce_sum.62
  102.0 12.1 %all-to-all-start.2 = ((bf16[8,64,128]{2,1,0:T(8,128)(2,1)}), bf16[8,64,128]{2,1,0:T(8,128)(2,1)S(1)}, u32[]{:S(2)}, u32[]{:S(2)}) async-start(bf16[8,64,128]{2,1,0:T(8,128)(2,1)} %bitcast.13), calls=%async_computation.2 | async-start | bytes 262144 | tf_op jit(solution)/shard_map/all_to_all | solution.py:209
  114.1 12.8 %all-gather.7.cloned.1.call-done = f32[256,16,128]{2,1,0:T(8,128)} async-done(((f32[16,16,128]{2,1,0:T(8,128)}), f32[256,16,128]{2,1,0:T(8,128)}) %all-gather.7.cloned.1.call-update) | async-done | bytes 2097168 | tf_op jit(solution)/shard_map/all_gather | solution.py:206
  126.9 0.8 constant_dynamic-slice_fusion
  127.8 0.0 copy-done.1
  127.8 0.6 fusion.2
  128.4 1.0 all-to-all-done.2
  129.4 0.6 copy.11
  (3 shorter events, 0.0 us)
Async XLA Ops:
  7.2 63.9 %all-gather.5.cloned.1.call-start = ((), (), s32[]{:S(2)}) async-start(), calls=%async_computation.3 | async-start | bytes 6266880 | tf_op jit(solution)/shard_map/all_gather | solution.py:193
  10.6 22.7 %all-to-all-start = ((f32[16,2,128]{2,1,0:T(2,128)}), f32[16,2,128]{2,1,0:T(2,128)S(1)}, u32[]{:S(2)}, u32[]{:S(2)}) async-start(f32[16,2,128]{2,1,0:T(2,128)} %bitcast.6), calls=%async_computation | async-start | bytes 32768 | tf_op jit(solution)/shard_map/all_to_all | solution.py:199
  27.0 100.0 %all-gather.7.cloned.1.call-start = ((), (), s32[]{:S(2)}) async-start(), calls=%async_computation.4 | async-start | bytes 2228224 | tf_op jit(solution)/shard_map/all_gather | solution.py:206
  33.3 0.6 copy-start
  79.9 47.9 %copy-start.1 = (s32[128,4]{0,1:T(4,128)S(1)}, s32[128,4]{0,1:T(4,128)}, u32[]{:S(2)}) copy-start(s32[128,4]{0,1:T(4,128)} %param.7) | copy-start | bytes 6148
  102.0 27.4 %all-to-all-start.2 = ((bf16[8,64,128]{2,1,0:T(8,128)(2,1)}), bf16[8,64,128]{2,1,0:T(8,128)(2,1)S(1)}, u32[]{:S(2)}, u32[]{:S(2)}) async-start(bf16[8,64,128]{2,1,0:T(8,128)(2,1)} %bitcast.13), calls=%async_computation.2 | async-start | bytes 262144 | tf_op jit(solution)/shard_map/all_to_all | solution.py:209
Sparse Core Ops, SparseCore 0:
  10.7 60.2 all-gather.4
  80.0 46.9 all-gather.6

commit v4 on v3

v4 whole, which is shorter than its diff:
```python
import functools

import jax
import jax.numpy as jnp
from jax import lax
from jax.experimental import pallas as pl
from jax.experimental.pallas import tpu as pltpu
from jax.sharding import Mesh, PartitionSpec as P

F32 = jnp.float32
BF16 = jnp.bfloat16
STEP = 4
SHIFT = 8
SPREAD = 16
FOLD = 4
LANE = 128
TILE = 256
VMEM = 56 * 1024 * 1024


def place_kernel(part_ref, meta_ref, h_ref, o_ref, hp_ref, op_ref, tall):
    odd = lax.rem(part_ref[0], 2)
    units, cap = h_ref.shape[1:]
    rows = hp_ref.shape[1] // FOLD
    slot_row = lax.broadcasted_iota(jnp.int32, (cap, cap), 0)
    gap = jnp.zeros((SHIFT, cap), F32)
    blank = jnp.zeros((rows - units // FOLD, cap), F32)
    for u in range(STEP):
        slot = meta_ref[u, 0:1, :].astype(jnp.int32)
        place = (slot_row == slot).astype(BF16)
        tall[...] = jnp.dot(h_ref[u], place, preferred_element_type=F32)
        out = jnp.dot(o_ref[u], place, preferred_element_type=F32)
        op_ref[u] = jnp.where(
            odd == 1, jnp.concatenate([gap, out], axis=0), jnp.concatenate([out, gap], axis=0)
        ).astype(BF16)
        for m in range(FOLD):
            picked = tall[pl.ds(m, units // FOLD, stride=FOLD), :]
            hp_ref[0, m * rows : (m + 1) * rows, u * cap : (u + 1) * cap] = jnp.concatenate(
                [picked, blank], axis=0
            ).astype(BF16)


def score_kernel(part_ref, g_ref, op_ref, s_ref, window, out, arrived):
    sources, width, _ = out.shape
    part = part_ref[0]
    start = pl.multiple_of(part * (width - SHIFT) - SHIFT * lax.rem(part, 2), 16)
    copies = []
    for i in range(sources // STEP):
        some = slice(i * STEP, (i + 1) * STEP)
        copies.append(
            (
                pltpu.make_async_copy(
                    g_ref.at[some, pl.ds(start, width), :], window.at[some], arrived.at[i, 0]
                ),
                pltpu.make_async_copy(op_ref.at[some], out.at[some], arrived.at[i, 1]),
            )
        )
    for pair in copies:
        for copy in pair:
            copy.start()
    for i, pair in enumerate(copies):
        for copy in pair:
            copy.wait()
        for u in range(i * STEP, (i + 1) * STEP):
            score = jnp.sum(out[u].astype(F32) * window[u].astype(F32), axis=0, keepdims=True)
            s_ref[u] = jnp.broadcast_to(score, s_ref.shape[1:])


def term_kernel(shape, meta_ref, g_ref, hp_ref, w_ref, acc, rhs, flat, grads, hidden, arrived):
    units, nx, nh, nl = shape
    sources, cols, cap = grads.shape
    wide = rhs.shape[0]
    copies = []
    for i in range(sources // STEP):
        copies.append([pltpu.make_async_copy(hp_ref.at[i], hidden.at[i], arrived.at[i, STEP])])
        for u in range(STEP):
            j = i * STEP + u
            copies[-1].append(pltpu.make_async_copy(g_ref.at[j], grads.at[j], arrived.at[i, u]))
    for group in copies:
        for copy in group:
            copy.start()
    rhs[cols:, :] = jnp.zeros((wide - cols, STEP * cap), BF16)
    for i, group in enumerate(copies):
        for copy in group:
            copy.wait()
        for u in range(STEP):
            j = i * STEP + u
            weight = meta_ref[j, 1:2, :]
            rhs[:cols, u * cap : (u + 1) * cap] = (grads[j].astype(F32) * weight).astype(BF16)
        for n in range(0, wide, TILE):
            term = lax.dot_general(
                hidden[i],
                rhs[n : n + TILE, :],
                (((1,), (1,)), ((), ())),
                preferred_element_type=F32,
            )
            acc[:, n : n + TILE] = term if i == 0 else acc[:, n : n + TILE] + term

    live, rows = units // FOLD, acc.shape[0] // FOLD
    span = FOLD * cols // LANE
    whole = units * cols // LANE
    flat[whole:, :] = jnp.zeros((flat.shape[0] - whole, LANE), F32)
    tail = None
    for m in range(FOLD):
        lead, offset = divmod(m * cols, LANE)
        lines = acc[m * rows : (m + 1) * rows, :]
        lines = pltpu.roll(lines, offset, 1) if offset else lines
        for t in range(wide // LANE):
            piece = lines[:live, t * LANE : (t + 1) * LANE]
            if t == 0 and offset:
                piece = piece + tail
            tail = piece
            end = (lead + t + 1) * LANE
            if end <= (m + 1) * cols:
                flat[pl.ds(lead + t, live, stride=span), :] = piece
            elif end - LANE < (m + 1) * cols:
                break
    size = w_ref.shape[1] // nh
    share = units * cols // (nx * nh * nl)
    lane = lax.broadcasted_iota(jnp.int32, (size, LANE), 1)
    for q in range(nx * nh * nl):
        x, z = divmod(q, nh * nl)
        base, offset = divmod(q * share, LANE)
        own = flat[base : base + size, :]
        if offset:
            after = flat[base + 1 : base + 1 + size, :]
            own = pltpu.roll(jnp.where(lane < offset, after, own), LANE - offset, 1)
        h, l = divmod(z, nl)
        w_ref[x * nl + l, h * size : (h + 1) * size, :] = own.astype(BF16)


def place(part, meta, h, o, rows):
    sources, units, cap = h.shape
    width = o.shape[1] + SHIFT
    return pl.pallas_call(
        place_kernel,
        grid_spec=pltpu.PrefetchScalarGridSpec(
            num_scalar_prefetch=1,
            grid=(sources // STEP,),
            in_specs=[
                pl.BlockSpec((STEP, 2, cap), lambda i, p: (i, 0, 0)),
                pl.BlockSpec((STEP, units, cap), lambda i, p: (i, 0, 0)),
                pl.BlockSpec((STEP, o.shape[1], cap), lambda i, p: (i, 0, 0)),
            ],
            out_specs=[
                pl.BlockSpec((1, FOLD * rows, STEP * cap), lambda i, p: (i, 0, 0)),
                pl.BlockSpec((STEP, width, cap), lambda i, p: (i, 0, 0)),
            ],
            scratch_shapes=[pltpu.VMEM((units, cap), F32)],
        ),
        out_shape=[
            jax.ShapeDtypeStruct((sources // STEP, FOLD * rows, STEP * cap), BF16),
            jax.ShapeDtypeStruct((sources, width, cap), BF16),
        ],
        compiler_params=pltpu.CompilerParams(vmem_limit_bytes=VMEM),
        cost_estimate=pl.CostEstimate(
            flops=4 * sources * units * cap * cap, bytes_accessed=8 * sources * units * cap, transcendentals=0
        ),
    )(part, meta, h, o)


def scores_of(part, g, op):
    sources, width, cap = op.shape
    return pl.pallas_call(
        score_kernel,
        in_specs=[
            pl.BlockSpec(memory_space=pltpu.SMEM),
            pl.BlockSpec(memory_space=pl.ANY),
            pl.BlockSpec(memory_space=pl.ANY),
        ],
        out_shape=jax.ShapeDtypeStruct((sources, SPREAD, cap), F32),
        scratch_shapes=[
            pltpu.VMEM((sources, width, cap), BF16),
            pltpu.VMEM((sources, width, cap), BF16),
            pltpu.SemaphoreType.DMA((sources // STEP, 2)),
        ],
        compiler_params=pltpu.CompilerParams(vmem_limit_bytes=VMEM),
        cost_estimate=pl.CostEstimate(
            flops=2 * sources * width * cap, bytes_accessed=4 * sources * width * cap, transcendentals=0
        ),
    )(part, g, op)


def weight_term(meta, g, hp, shape):
    units, nx, nh, nl = shape
    sources, cols, cap = g.shape
    high = hp.shape[1]
    wide = -(-cols // TILE) * TILE
    share = units * cols // (nx * nh * nl)
    size = -(-share // (16 * LANE)) * 16
    lines = -(-((nx * nh * nl - 1) * share // LANE + size + 1) // 8) * 8
    return pl.pallas_call(
        functools.partial(term_kernel, shape),
        in_specs=[
            pl.BlockSpec(memory_space=pltpu.VMEM),
            pl.BlockSpec(memory_space=pl.ANY),
            pl.BlockSpec(memory_space=pl.ANY),
        ],
        out_specs=pl.BlockSpec(memory_space=pltpu.VMEM),
        out_shape=jax.ShapeDtypeStruct((nx * nl, nh * size, LANE), BF16),
        scratch_shapes=[
            pltpu.VMEM((high, wide), F32),
            pltpu.VMEM((wide, STEP * cap), BF16),
            pltpu.VMEM((lines, LANE), F32),
            pltpu.VMEM((sources, cols, cap), BF16),
            pltpu.VMEM(hp.shape, BF16),
            pltpu.SemaphoreType.DMA((sources // STEP, STEP + 1)),
        ],
        compiler_params=pltpu.CompilerParams(vmem_limit_bytes=VMEM),
        cost_estimate=pl.CostEstimate(
            flops=2 * sources * cap * high * wide, bytes_accessed=2 * sources * cols * cap, transcendentals=0
        ),
    )(meta, g, hp)


def local(out_grad, routes, slots, combine_weight, saved_hidden, saved_out):
    nx, nh, nl = (lax.axis_size(name) for name in ("x", "zh", "zl"))
    blocks = lax.axis_size("y") * lax.axis_size("c")
    cap, units = saved_hidden.shape[3:]
    cols = out_grad.shape[1]
    split = cols // saved_out.shape[4]
    experts = blocks // split
    me = lax.axis_index("y") * lax.axis_size("c") + lax.axis_index("c")
    part = (me % split).reshape(1).astype(jnp.int32)
    rows = -(-(units // FOLD) // 16) * 16

    gathered = lax.all_gather(out_grad.T, ("y", "c"), axis=0)

    names = routes.T[None] == jnp.arange(experts, dtype=jnp.int32)[:, None, None]
    slot_of = jnp.sum(jnp.where(names, slots.T[None].astype(F32), 0.0), axis=1)
    weight_of = jnp.sum(jnp.where(names, combine_weight.T[None].astype(F32), 0.0), axis=1)
    sent = jnp.repeat(jnp.stack([slot_of, weight_of], axis=1), split, axis=0)
    meta = lax.all_to_all(sent, ("y", "c"), split_axis=0, concat_axis=0, tiled=True)

    h = saved_hidden[0, 0].transpose(0, 2, 1)
    o = saved_out[0, 0].transpose(0, 2, 1)
    hp, op = place(part, meta, h, o, rows)
    scores = scores_of(part, gathered, op)
    gathered, scores = lax.optimization_barrier((gathered, scores))
    everyones = lax.all_gather(scores, ("y", "c"), axis=0)
    term = weight_term(meta, gathered, hp, (units, nx, nh, nl))
    first = lax.all_to_all(term, ("x", "zl"), split_axis=0, concat_axis=0, tiled=True)
    partial_sum = jnp.sum(first.astype(F32), axis=0).astype(BF16)
    second = lax.all_to_all(
        partial_sum.reshape(nh, -1, LANE), "zh", split_axis=0, concat_axis=0, tiled=True
    )
    summed = jnp.sum(second.astype(F32), axis=0).astype(BF16)
    weight_grad = summed.reshape(1, -1)[:, : units * cols // (nx * nh * nl)]

    returned = lax.dynamic_slice_in_dim(everyones, me, 1, axis=1)[:, 0, 0]
    combined = jnp.sum(returned.reshape(experts, split, cap), axis=1)
    router_grad = jnp.sum(jnp.where(names, combined[:, None, :], 0.0), axis=0).T
    return (weight_grad, router_grad)


def solution(mesh):
    nx = {64: 4, 4: 2}[mesh.shape["dp"]]
    grid = Mesh(
        mesh.devices.reshape(nx, mesh.shape["dp"] // nx // 2, 2, mesh.shape["expert"] // 2, 2),
        ("x", "zh", "zl", "y", "c"),
    )
    rows = P(("x", "zh", "zl", "y", "c"), None)
    saved = P(("x", "zh", "zl"), ("y", "c"), None, None, None)
    return jax.shard_map(
        local,
        mesh=grid,
        in_specs=(rows, rows, rows, rows, saved, saved),
        out_specs=(P(("y", "c"), ("x", "zh", "zl")), rows),
        check_vma=False,
    )
```

time: 137 us -> 138 us (level)
    all_gather x1, waiting for transfers between devices: 12.8 us -> 5.63 us  [local(): everyones = lax.all_gather(scores, ('y', 'c'), axis=0)]
    all_to_all x1, waiting for transfers between devices: 1.02 us -> 8.17 us  [local(): lax.all_to_all(partial_sum.reshape(nh, -1, LANE), 'zh', split_axis=0, con...]
    pallas_call x1 -> x2, Pallas kernels: 8.82 us -> 9.51 us  [the longest x1 6.81 us: weight_term(): pl.pallas_call(functools.partial(term_kernel, shape), in_specs=[pl.BlockS...]
  transfers between devices with their start and end apart: 4 -> 4, of which waited for: 4 -> 4; matrix products, arithmetic and copies ran while one was open for 4% -> 4% of each run, Pallas kernels for 4% -> 9%
where the time goes in v4:
time: 138 us
  waiting for transfers between devices  52.6 us (38%)
  starting transfers between devices  28.6 us (21%)
  blocking collectives  21.3 us (15%)
  Pallas kernels  14.8 us (11%)
  between operations  14.1 us (10%)
  other arithmetic  3.5 us (3%)
  local copies, waits for them, and re-layouts  2.71 us (2%)
    all_gather x1, waiting for transfers between devices, local(): gathered = lax.all_gather(out_grad.T, ('y', 'c'), axis=0)  31.9 us
    all_to_all x1, blocking collectives, local(): lax.all_to_all(term, ('x', 'zl'), split_axis=0, concat_axis=0, tiled=True)  21.3 us
    all_to_all x1, starting transfers between devices, local(): lax.all_to_all(sent, ('y', 'c'), split_axis=0, concat_axis=0, tiled=True)  16.4 us
    all_to_all x1, starting transfers between devices, local(): lax.all_to_all(partial_sum.reshape(nh, -1, LANE), 'zh', split_axis=0, con...  12.1 us
    all_to_all x1, waiting for transfers between devices, local(): lax.all_to_all(partial_sum.reshape(nh, -1, LANE), 'zh', split_axis=0, con...  8.17 us
    pallas_call x1, Pallas kernels, weight_term(): pl.pallas_call(functools.partial(term_kernel, shape), in_specs=[pl.BlockS...  6.81 us
    all_to_all x1, waiting for transfers between devices, local(): lax.all_to_all(sent, ('y', 'c'), split_axis=0, concat_axis=0, tiled=True)  6.22 us
    all_gather x1, waiting for transfers between devices, local(): everyones = lax.all_gather(scores, ('y', 'c'), axis=0)  5.63 us
  transfers between devices with their start and end apart: 4, of which 4 were waited for; matrix products, arithmetic and copies ran while one was open for 4% of the time, Pallas kernels for 9%

profile of v4, /device:TPU:8, one launch (start us, length us, event | category | flops | bytes accessed | tf_op | source)
XLA Modules:
  0.0 137.5 jit_solution(16716327702462901470)
XLA Ops:
  7.2 0.0 all-gather.5.cloned.1.call-start
  7.2 0.7 all-gather.5.cloned.1.call-update
  7.9 0.7 convert_bitcast_fusion
  8.6 0.7 convert_bitcast_fusion.1
  9.3 0.7 select_reduce_fusion.1
  10.0 0.6 broadcast_in_dim.39
  10.6 16.4 %all-to-all-start = ((f32[16,2,128]{2,1,0:T(2,128)}), f32[16,2,128]{2,1,0:T(2,128)S(1)}, u32[]{:S(2)}, u32[]{:S(2)}) async-start(f32[16,2,128]{2,1,0:T(2,128)} %bitcast.5), calls=%async_computation | async-start | bytes 32768 | tf_op jit(solution)/shard_map/all_to_all | solution.py:233
  27.0 0.0 all-gather.7.cloned.1.call-start
  27.0 6.2 %all-to-all-done.meta_ref = f32[16,2,128]{2,1,0:T(2,128)S(1)} async-done(((f32[16,2,128]{2,1,0:T(2,128)}), f32[16,2,128]{2,1,0:T(2,128)S(1)}, u32[]{:S(2)}, u32[]{:S(2)}) %all-to-all-start) | async-done | bytes 16416 | tf_op jit(solution)/shard_map/all_to_all | solution.py:233
  33.3 0.0 copy-start
  33.3 0.6 copy-done
  33.9 5.3 %shard_map.77 = (bf16[4,384,512]{2,1,0:T(8,128)(2,1)}, bf16[16,368,128]{2,1,0:T(8,128)(2,1)}) custom-call(s32[1]{0:T(128)} %bitcast.8.part_ref, f32[16,2,128]{2,1,0:T(2,128)} %copy-done, bf16[16,360,128]{2,1,0:T(8,128)(2,1)} %bitcast.30, bf16[16,360,128]{2,1,0:T(8,128)(2,1)} %bitcast.31), custom_call_target="tpu_custom_call" | custom-call | flops 377487360 | bytes 5898240 | tf_op jit(solution)/shard_map/pallas_call | solution.py:135
  39.2 31.9 %all-gather.5.cloned.1.call-done = bf16[23040,128]{1,0:T(8,128)(2,1)} async-done(((bf16[1440,128]{1,0:T(8,128)(2,1)}), bf16[23040,128]{1,0:T(8,128)(2,1)}) %all-gather.5.cloned.1.call-update) | async-done | bytes 5898256 | tf_op jit(solution)/shard_map/all_gather | solution.py:227
  71.0 2.7 %shard_map.78 = f32[16,16,128]{2,1,0:T(8,128)} custom-call(s32[1]{0:T(128)} %bitcast.8.part_ref, bf16[16,1440,128]{2,1,0:T(8,128)(2,1)} %bitcast.28, bf16[16,368,128]{2,1,0:T(8,128)(2,1)} %get-tuple-element.6.op_ref), custom_call_target="tpu_custom_call" | custom-call | flops 1507328 | bytes 3014656 | tf_op jit(solution)/shard_map/pallas_call | solution.py:164
  73.7 0.0 all-gather.7.cloned.1.call-update
  73.8 6.8 %shard_map.79 = bf16[8,512,128]{2,1,0:T(8,128)(2,1)} custom-call(f32[16,2,128]{2,1,0:T(2,128)} %copy-done, bf16[16,1440,128]{2,1,0:T(8,128)(2,1)} %bitcast.29, bf16[4,384,512]{2,1,0:T(8,128)(2,1)} %get-tuple-element.8.hp_ref), custom_call_target="tpu_custom_call" | custom-call | flops 2415919104 | bytes 5898240 | tf_op jit(solution)/shard_map/pallas_call | solution.py:192
  80.6 0.0 copy-start.1
  80.6 21.3 %all_to_all.15 = bf16[8,512,128]{2,1,0:T(8,128)(2,1)S(1)} all-to-all(bf16[8,512,128]{2,1,0:T(8,128)(2,1)} %shard_map.79), channel_id=1, replica_groups=mesh['x'=4,'zh'=8,'zl'=2,'y'=8,'c'=2] {'x','zl'}, dimensions={0} | all-to-all | bytes 2097152 | tf_op jit(solution)/shard_map/all_to_all | solution.py:242
  101.9 0.8 reduce_sum.62
  102.7 12.1 %all-to-all-start.2 = ((bf16[8,64,128]{2,1,0:T(8,128)(2,1)}), bf16[8,64,128]{2,1,0:T(8,128)(2,1)S(1)}, u32[]{:S(2)}, u32[]{:S(2)}) async-start(bf16[8,64,128]{2,1,0:T(8,128)(2,1)} %bitcast.13), calls=%async_computation.2 | async-start | bytes 262144 | tf_op jit(solution)/shard_map/all_to_all | solution.py:244
  114.8 5.6 %all-gather.7.cloned.1.call-done = f32[256,16,128]{2,1,0:T(8,128)} async-done(((f32[16,16,128]{2,1,0:T(8,128)}), f32[256,16,128]{2,1,0:T(8,128)}) %all-gather.7.cloned.1.call-update) | async-done | bytes 2097168 | tf_op jit(solution)/shard_map/all_gather | solution.py:240
  120.4 0.8 constant_dynamic-slice_fusion
  121.3 0.0 copy-done.1
  121.3 0.6 fusion.2
  121.9 8.2 %all-to-all-done.2 = bf16[8,64,128]{2,1,0:T(8,128)(2,1)S(1)} async-done(((bf16[8,64,128]{2,1,0:T(8,128)(2,1)}), bf16[8,64,128]{2,1,0:T(8,128)(2,1)S(1)}, u32[]{:S(2)}, u32[]{:S(2)}) %all-to-all-start.2) | async-done | bytes 131104 | tf_op jit(solution)/shard_map/all_to_all | solution.py:244
  130.1 0.6 copy.11
  (3 shorter events, 0.0 us)
Async XLA Ops:
  7.2 63.9 %all-gather.5.cloned.1.call-start = ((), (), s32[]{:S(2)}) async-start(), calls=%async_computation.3 | async-start | bytes 6266880 | tf_op jit(solution)/shard_map/all_gather | solution.py:227
  10.6 22.7 %all-to-all-start = ((f32[16,2,128]{2,1,0:T(2,128)}), f32[16,2,128]{2,1,0:T(2,128)S(1)}, u32[]{:S(2)}, u32[]{:S(2)}) async-start(f32[16,2,128]{2,1,0:T(2,128)} %bitcast.5), calls=%async_computation | async-start | bytes 32768 | tf_op jit(solution)/shard_map/all_to_all | solution.py:233
  27.0 93.4 %all-gather.7.cloned.1.call-start = ((), (), s32[]{:S(2)}) async-start(), calls=%async_computation.4 | async-start | bytes 2228224 | tf_op jit(solution)/shard_map/all_gather | solution.py:240
  33.3 0.6 copy-start
  80.6 40.7 %copy-start.1 = (s32[128,4]{0,1:T(4,128)S(1)}, s32[128,4]{0,1:T(4,128)}, u32[]{:S(2)}) copy-start(s32[128,4]{0,1:T(4,128)} %param.7) | copy-start | bytes 6148
  102.7 27.4 %all-to-all-start.2 = ((bf16[8,64,128]{2,1,0:T(8,128)(2,1)}), bf16[8,64,128]{2,1,0:T(8,128)(2,1)S(1)}, u32[]{:S(2)}, u32[]{:S(2)}) async-start(bf16[8,64,128]{2,1,0:T(8,128)(2,1)} %bitcast.13), calls=%async_computation.2 | async-start | bytes 262144 | tf_op jit(solution)/shard_map/all_to_all | solution.py:244
Sparse Core Ops, SparseCore 0:
  10.7 60.2 all-gather.4
  73.9 46.4 all-gather.6

commit v5 on v4

--- a/solution.py
+++ b/solution.py
@@ -40,34 +40,14 @@
             ).astype(BF16)
 
 
-def score_kernel(part_ref, g_ref, op_ref, s_ref, window, out, arrived):
-    sources, width, _ = out.shape
+def term_kernel(
+    shape, part_ref, meta_ref, g_ref, hp_ref, op_ref, w_ref, s_ref,
+    acc, rhs, flat, grads, hidden, out, owned, arrived, left,
+):
+    units, nx, nh, nl = shape
     part = part_ref[0]
+    width = out.shape[1]
     start = pl.multiple_of(part * (width - SHIFT) - SHIFT * lax.rem(part, 2), 16)
-    copies = []
-    for i in range(sources // STEP):
-        some = slice(i * STEP, (i + 1) * STEP)
-        copies.append(
-            (
-                pltpu.make_async_copy(
-                    g_ref.at[some, pl.ds(start, width), :], window.at[some], arrived.at[i, 0]
-                ),
-                pltpu.make_async_copy(op_ref.at[some], out.at[some], arrived.at[i, 1]),
-            )
-        )
-    for pair in copies:
-        for copy in pair:
-            copy.start()
-    for i, pair in enumerate(copies):
-        for copy in pair:
-            copy.wait()
-        for u in range(i * STEP, (i + 1) * STEP):
-            score = jnp.sum(out[u].astype(F32) * window[u].astype(F32), axis=0, keepdims=True)
-            s_ref[u] = jnp.broadcast_to(score, s_ref.shape[1:])
-
-
-def term_kernel(shape, meta_ref, g_ref, hp_ref, w_ref, acc, rhs, flat, grads, hidden, arrived):
-    units, nx, nh, nl = shape
     sources, cols, cap = grads.shape
     wide = rhs.shape[0]
     copies = []
@@ -76,6 +56,10 @@
         for u in range(STEP):
             j = i * STEP + u
             copies[-1].append(pltpu.make_async_copy(g_ref.at[j], grads.at[j], arrived.at[i, u]))
+        some = slice(i * STEP, (i + 1) * STEP)
+        copies[-1].append(
+            pltpu.make_async_copy(op_ref.at[some], out.at[some], arrived.at[i, STEP + 1])
+        )
     for group in copies:
         for copy in group:
             copy.start()
@@ -86,6 +70,9 @@
         for u in range(STEP):
             j = i * STEP + u
             weight = meta_ref[j, 1:2, :]
+            window = grads[j, pl.ds(start, width), :].astype(F32)
+            score = jnp.sum(out[j].astype(F32) * window, axis=0, keepdims=True)
+            s_ref[j] = jnp.broadcast_to(score, s_ref.shape[1:])
             rhs[:cols, u * cap : (u + 1) * cap] = (grads[j].astype(F32) * weight).astype(BF16)
         for n in range(0, wide, TILE):
             term = lax.dot_general(
@@ -115,18 +102,23 @@
                 flat[pl.ds(lead + t, live, stride=span), :] = piece
             elif end - LANE < (m + 1) * cols:
                 break
-    size = w_ref.shape[1] // nh
+    size = owned.shape[1] // nh
     share = units * cols // (nx * nh * nl)
     lane = lax.broadcasted_iota(jnp.int32, (size, LANE), 1)
-    for q in range(nx * nh * nl):
-        x, z = divmod(q, nh * nl)
-        base, offset = divmod(q * share, LANE)
-        own = flat[base : base + size, :]
-        if offset:
-            after = flat[base + 1 : base + 1 + size, :]
-            own = pltpu.roll(jnp.where(lane < offset, after, own), LANE - offset, 1)
-        h, l = divmod(z, nl)
-        w_ref[x * nl + l, h * size : (h + 1) * size, :] = own.astype(BF16)
+    leaving = []
+    for dest in range(nx * nl):
+        x, l = divmod(dest, nl)
+        for h in range(nh):
+            base, offset = divmod(((x * nh + h) * nl + l) * share, LANE)
+            own = flat[base : base + size, :]
+            if offset:
+                after = flat[base + 1 : base + 1 + size, :]
+                own = pltpu.roll(jnp.where(lane < offset, after, own), LANE - offset, 1)
+            owned[dest, h * size : (h + 1) * size, :] = own.astype(BF16)
+        leaving.append(pltpu.make_async_copy(owned.at[dest], w_ref.at[dest], left.at[dest]))
+        leaving[-1].start()
+    for copy in leaving:
+        copy.wait()
 
 
 def place(part, meta, h, o, rows):
@@ -159,29 +151,7 @@
     )(part, meta, h, o)
 
 
-def scores_of(part, g, op):
-    sources, width, cap = op.shape
-    return pl.pallas_call(
-        score_kernel,
-        in_specs=[
-            pl.BlockSpec(memory_space=pltpu.SMEM),
-            pl.BlockSpec(memory_space=pl.ANY),
-            pl.BlockSpec(memory_space=pl.ANY),
-        ],
-        out_shape=jax.ShapeDtypeStruct((sources, SPREAD, cap), F32),
-        scratch_shapes=[
-            pltpu.VMEM((sources, width, cap), BF16),
-            pltpu.VMEM((sources, width, cap), BF16),
-            pltpu.SemaphoreType.DMA((sources // STEP, 2)),
-        ],
-        compiler_params=pltpu.CompilerParams(vmem_limit_bytes=VMEM),
-        cost_estimate=pl.CostEstimate(
-            flops=2 * sources * width * cap, bytes_accessed=4 * sources * width * cap, transcendentals=0
-        ),
-    )(part, g, op)
-
-
-def weight_term(meta, g, hp, shape):
+def weight_term(part, meta, g, hp, op, shape):
     units, nx, nh, nl = shape
     sources, cols, cap = g.shape
     high = hp.shape[1]
@@ -192,25 +162,36 @@
     return pl.pallas_call(
         functools.partial(term_kernel, shape),
         in_specs=[
+            pl.BlockSpec(memory_space=pltpu.SMEM),
             pl.BlockSpec(memory_space=pltpu.VMEM),
             pl.BlockSpec(memory_space=pl.ANY),
             pl.BlockSpec(memory_space=pl.ANY),
-        ],
-        out_specs=pl.BlockSpec(memory_space=pltpu.VMEM),
-        out_shape=jax.ShapeDtypeStruct((nx * nl, nh * size, LANE), BF16),
+            pl.BlockSpec(memory_space=pl.ANY),
+        ],
+        out_specs=[
+            pl.BlockSpec(memory_space=pl.ANY),
+            pl.BlockSpec(memory_space=pltpu.VMEM),
+        ],
+        out_shape=[
+            jax.ShapeDtypeStruct((nx * nl, nh * size, LANE), BF16),
+            jax.ShapeDtypeStruct((sources, SPREAD, cap), F32),
+        ],
         scratch_shapes=[
             pltpu.VMEM((high, wide), F32),
             pltpu.VMEM((wide, STEP * cap), BF16),
             pltpu.VMEM((lines, LANE), F32),
             pltpu.VMEM((sources, cols, cap), BF16),
             pltpu.VMEM(hp.shape, BF16),
-            pltpu.SemaphoreType.DMA((sources // STEP, STEP + 1)),
+            pltpu.VMEM(op.shape, BF16),
+            pltpu.VMEM((nx * nl, nh * size, LANE), BF16),
+            pltpu.SemaphoreType.DMA((sources // STEP, STEP + 2)),
+            pltpu.SemaphoreType.DMA((nx * nl,)),
         ],
         compiler_params=pltpu.CompilerParams(vmem_limit_bytes=VMEM),
         cost_estimate=pl.CostEstimate(
             flops=2 * sources * cap * high * wide, bytes_accessed=2 * sources * cols * cap, transcendentals=0
         ),
-    )(meta, g, hp)
+    )(part, meta, g, hp, op)
 
 
 def local(out_grad, routes, slots, combine_weight, saved_hidden, saved_out):
@@ -235,21 +216,21 @@
     h = saved_hidden[0, 0].transpose(0, 2, 1)
     o = saved_out[0, 0].transpose(0, 2, 1)
     hp, op = place(part, meta, h, o, rows)
-    scores = scores_of(part, gathered, op)
-    gathered, scores = lax.optimization_barrier((gathered, scores))
+    term, scores = weight_term(part, meta, gathered, hp, op, (units, nx, nh, nl))
     everyones = lax.all_gather(scores, ("y", "c"), axis=0)
-    term = weight_term(meta, gathered, hp, (units, nx, nh, nl))
+
     first = lax.all_to_all(term, ("x", "zl"), split_axis=0, concat_axis=0, tiled=True)
     partial_sum = jnp.sum(first.astype(F32), axis=0).astype(BF16)
     second = lax.all_to_all(
         partial_sum.reshape(nh, -1, LANE), "zh", split_axis=0, concat_axis=0, tiled=True
     )
-    summed = jnp.sum(second.astype(F32), axis=0).astype(BF16)
-    weight_grad = summed.reshape(1, -1)[:, : units * cols // (nx * nh * nl)]
-
     returned = lax.dynamic_slice_in_dim(everyones, me, 1, axis=1)[:, 0, 0]
     combined = jnp.sum(returned.reshape(experts, split, cap), axis=1)
     router_grad = jnp.sum(jnp.where(names, combined[:, None, :], 0.0), axis=0).T
+    second, router_grad = lax.optimization_barrier((second, router_grad))
+
+    summed = jnp.sum(second.astype(F32), axis=0).astype(BF16)
+    weight_grad = summed.reshape(1, -1)[:, : units * cols // (nx * nh * nl)]
     return (weight_grad, router_grad)
 
 

time: 138 us -> 137 us (level)
    all_gather x1, waiting for transfers between devices: 5.63 us -> 12.8 us  [local(): everyones = lax.all_gather(scores, ('y', 'c'), axis=0)]
    all_to_all x1, waiting for transfers between devices: 8.17 us -> 1.05 us  [local(): lax.all_to_all(partial_sum.reshape(nh, -1, LANE), 'zh', split_axis=0, con...]
    pallas_call x1 -> x0, Pallas kernels: 2.7 us -> none  [scores_of(): pl.pallas_call(score_kernel, in_specs=[pl.BlockSpec(memory_space=pltpu.SM...]
  transfers between devices with their start and end apart: 4 -> 4, of which waited for: 4 -> 4; matrix products, arithmetic and copies ran while one was open for 4% -> 4% of each run, Pallas kernels for 9% -> 4%
where the time goes in v5:
time: 137 us; the launch traced here: 136 us
  waiting for transfers between devices  52.6 us (38%)
  starting transfers between devices  28.6 us (21%)
  blocking collectives  21.4 us (16%)
  between operations  14.1 us (10%)
  Pallas kernels  13.5 us (10%)
  other arithmetic  3.5 us (3%)
  local copies, waits for them, and re-layouts  2.71 us (2%)
    all_gather x1, waiting for transfers between devices, local(): gathered = lax.all_gather(out_grad.T, ('y', 'c'), axis=0)  31.9 us
    all_to_all x1, blocking collectives, local(): lax.all_to_all(term, ('x', 'zl'), split_axis=0, concat_axis=0, tiled=True)  21.4 us
    all_to_all x1, starting transfers between devices, local(): lax.all_to_all(sent, ('y', 'c'), split_axis=0, concat_axis=0, tiled=True)  16.4 us
    all_gather x1, waiting for transfers between devices, local(): everyones = lax.all_gather(scores, ('y', 'c'), axis=0)  12.8 us
    all_to_all x1, starting transfers between devices, local(): lax.all_to_all(partial_sum.reshape(nh, -1, LANE), 'zh', split_axis=0, con...  12.1 us
    pallas_call x1, Pallas kernels, weight_term(): pl.pallas_call(functools.partial(term_kernel, shape), in_specs=[pl.BlockS...  8.17 us
    all_to_all x1, waiting for transfers between devices, local(): lax.all_to_all(sent, ('y', 'c'), split_axis=0, concat_axis=0, tiled=True)  6.22 us
    pallas_call x1, Pallas kernels, place(): pl.pallas_call(place_kernel, grid_spec=pltpu.PrefetchScalarGridSpec(num_s...  5.28 us
  transfers between devices with their start and end apart: 4, of which 4 were waited for; matrix products, arithmetic and copies ran while one was open for 4% of the time, Pallas kernels for 4%

profile of v5, /device:TPU:8, one launch (start us, length us, event | category | flops | bytes accessed | tf_op | source)
XLA Modules:
  0.0 136.3 jit_solution(17604442374502480298)
XLA Ops:
  7.2 0.0 all-gather.5.cloned.1.call-start
  7.2 0.7 all-gather.5.cloned.1.call-update
  7.9 0.7 convert_bitcast_fusion
  8.6 0.7 convert_bitcast_fusion.1
  9.3 0.7 select_reduce_fusion.1
  10.0 0.6 broadcast_in_dim.39
  10.6 16.4 %all-to-all-start = ((f32[16,2,128]{2,1,0:T(2,128)}), f32[16,2,128]{2,1,0:T(2,128)S(1)}, u32[]{:S(2)}, u32[]{:S(2)}) async-start(f32[16,2,128]{2,1,0:T(2,128)} %bitcast.6), calls=%async_computation | async-start | bytes 32768 | tf_op jit(solution)/shard_map/all_to_all | solution.py:214
  27.0 0.0 all-gather.7.cloned.1.call-start
  27.0 6.2 %all-to-all-done.meta_ref = f32[16,2,128]{2,1,0:T(2,128)S(1)} async-done(((f32[16,2,128]{2,1,0:T(2,128)}), f32[16,2,128]{2,1,0:T(2,128)S(1)}, u32[]{:S(2)}, u32[]{:S(2)}) %all-to-all-start) | async-done | bytes 16416 | tf_op jit(solution)/shard_map/all_to_all | solution.py:214
  33.3 0.0 copy-start
  33.3 0.6 copy-done
  33.9 5.3 %shard_map.77 = (bf16[4,384,512]{2,1,0:T(8,128)(2,1)}, bf16[16,368,128]{2,1,0:T(8,128)(2,1)}) custom-call(s32[1]{0:T(128)} %bitcast.part_ref, f32[16,2,128]{2,1,0:T(2,128)} %copy-done, bf16[16,360,128]{2,1,0:T(8,128)(2,1)} %bitcast.29, bf16[16,360,128]{2,1,0:T(8,128)(2,1)} %bitcast.30), custom_call_target="tpu_custom_call" | custom-call | flops 377487360 | bytes 5898240 | tf_op jit(solution)/shard_map/pallas_call | solution.py:127
  39.2 31.9 %all-gather.5.cloned.1.call-done = bf16[23040,128]{1,0:T(8,128)(2,1)} async-done(((bf16[1440,128]{1,0:T(8,128)(2,1)}), bf16[23040,128]{1,0:T(8,128)(2,1)}) %all-gather.5.cloned.1.call-update) | async-done | bytes 5898256 | tf_op jit(solution)/shard_map/all_gather | solution.py:208
  71.0 8.2 %shard_map.78 = (bf16[8,512,128]{2,1,0:T(8,128)(2,1)}, f32[16,16,128]{2,1,0:T(8,128)}) custom-call(s32[1]{0:T(128)} %bitcast.part_ref, f32[16,2,128]{2,1,0:T(2,128)} %copy-done, bf16[16,1440,128]{2,1,0:T(8,128)(2,1)} %bitcast.28, bf16[4,384,512]{2,1,0:T(8,128)(2,1)} %get-tuple-element.8.hp_ref, bf16[16,368,128]{2,1,0:T(8,128)(2,1)} %get-tuple-element.9.op_ref), custom_call_target="tpu_custom_call" | custom-call | flops 2415919104 | bytes 5898240 | tf_op jit(solution)/shard_map/pallas_call | solution.py:162
  79.2 0.0 all-gather.7.cloned.1.call-update
  79.2 0.0 copy-start.1
  79.2 21.4 %all_to_all.15 = bf16[8,512,128]{2,1,0:T(8,128)(2,1)S(1)} all-to-all(bf16[8,512,128]{2,1,0:T(8,128)(2,1)} %get-tuple-element.10), channel_id=1, replica_groups=mesh['x'=4,'zh'=8,'zl'=2,'y'=8,'c'=2] {'x','zl'}, dimensions={0} | all-to-all | bytes 2097152 | tf_op jit(solution)/shard_map/all_to_all | solution.py:222
  100.6 0.8 reduce_sum.62
  101.4 12.1 %all-to-all-start.2 = ((bf16[8,64,128]{2,1,0:T(8,128)(2,1)}), bf16[8,64,128]{2,1,0:T(8,128)(2,1)S(1)}, u32[]{:S(2)}, u32[]{:S(2)}) async-start(bf16[8,64,128]{2,1,0:T(8,128)(2,1)} %bitcast.13), calls=%async_computation.2 | async-start | bytes 262144 | tf_op jit(solution)/shard_map/all_to_all | solution.py:224
  113.5 12.8 %all-gather.7.cloned.1.call-done = f32[256,16,128]{2,1,0:T(8,128)} async-done(((f32[16,16,128]{2,1,0:T(8,128)}), f32[256,16,128]{2,1,0:T(8,128)}) %all-gather.7.cloned.1.call-update) | async-done | bytes 2097168 | tf_op jit(solution)/shard_map/all_gather | solution.py:220
  126.3 0.8 constant_dynamic-slice_fusion
  127.2 0.0 copy-done.1
  127.2 0.6 fusion.2
  127.8 1.1 all-to-all-done.2
  128.8 0.6 copy.11
  (3 shorter events, 0.0 us)
Async XLA Ops:
  7.2 63.9 %all-gather.5.cloned.1.call-start = ((), (), s32[]{:S(2)}) async-start(), calls=%async_computation.3 | async-start | bytes 6266880 | tf_op jit(solution)/shard_map/all_gather | solution.py:208
  10.6 22.7 %all-to-all-start = ((f32[16,2,128]{2,1,0:T(2,128)}), f32[16,2,128]{2,1,0:T(2,128)S(1)}, u32[]{:S(2)}, u32[]{:S(2)}) async-start(f32[16,2,128]{2,1,0:T(2,128)} %bitcast.6), calls=%async_computation | async-start | bytes 32768 | tf_op jit(solution)/shard_map/all_to_all | solution.py:214
  27.0 99.3 %all-gather.7.cloned.1.call-start = ((), (), s32[]{:S(2)}) async-start(), calls=%async_computation.4 | async-start | bytes 2228224 | tf_op jit(solution)/shard_map/all_gather | solution.py:220
  33.3 0.6 copy-start
  79.2 47.9 %copy-start.1 = (s32[128,4]{0,1:T(4,128)S(1)}, s32[128,4]{0,1:T(4,128)}, u32[]{:S(2)}) copy-start(s32[128,4]{0,1:T(4,128)} %param.7) | copy-start | bytes 6148
  101.4 27.4 %all-to-all-start.2 = ((bf16[8,64,128]{2,1,0:T(8,128)(2,1)}), bf16[8,64,128]{2,1,0:T(8,128)(2,1)S(1)}, u32[]{:S(2)}, u32[]{:S(2)}) async-start(bf16[8,64,128]{2,1,0:T(8,128)(2,1)} %bitcast.13), calls=%async_computation.2 | async-start | bytes 262144 | tf_op jit(solution)/shard_map/all_to_all | solution.py:224
Sparse Core Ops, SparseCore 0:
  10.7 60.2 all-gather.4
  79.4 46.9 all-gather.6

commit v6 on v4

--- a/solution.py
+++ b/solution.py
@@ -66,7 +66,9 @@
             s_ref[u] = jnp.broadcast_to(score, s_ref.shape[1:])
 
 
-def term_kernel(shape, meta_ref, g_ref, hp_ref, w_ref, acc, rhs, flat, grads, hidden, arrived):
+def term_kernel(
+    shape, meta_ref, g_ref, hp_ref, w_ref, acc, rhs, flat, grads, hidden, owned, arrived, left
+):
     units, nx, nh, nl = shape
     sources, cols, cap = grads.shape
     wide = rhs.shape[0]
@@ -115,18 +117,23 @@
                 flat[pl.ds(lead + t, live, stride=span), :] = piece
             elif end - LANE < (m + 1) * cols:
                 break
-    size = w_ref.shape[1] // nh
+    size = owned.shape[1] // nh
     share = units * cols // (nx * nh * nl)
     lane = lax.broadcasted_iota(jnp.int32, (size, LANE), 1)
-    for q in range(nx * nh * nl):
-        x, z = divmod(q, nh * nl)
-        base, offset = divmod(q * share, LANE)
-        own = flat[base : base + size, :]
-        if offset:
-            after = flat[base + 1 : base + 1 + size, :]
-            own = pltpu.roll(jnp.where(lane < offset, after, own), LANE - offset, 1)
-        h, l = divmod(z, nl)
-        w_ref[x * nl + l, h * size : (h + 1) * size, :] = own.astype(BF16)
+    leaving = []
+    for dest in range(nx * nl):
+        x, l = divmod(dest, nl)
+        for h in range(nh):
+            base, offset = divmod(((x * nh + h) * nl + l) * share, LANE)
+            own = flat[base : base + size, :]
+            if offset:
+                after = flat[base + 1 : base + 1 + size, :]
+                own = pltpu.roll(jnp.where(lane < offset, after, own), LANE - offset, 1)
+            owned[dest, h * size : (h + 1) * size, :] = own.astype(BF16)
+        leaving.append(pltpu.make_async_copy(owned.at[dest], w_ref.at[dest], left.at[dest]))
+        leaving[-1].start()
+    for copy in leaving:
+        copy.wait()
 
 
 def place(part, meta, h, o, rows):
@@ -152,7 +159,7 @@
             jax.ShapeDtypeStruct((sources // STEP, FOLD * rows, STEP * cap), BF16),
             jax.ShapeDtypeStruct((sources, width, cap), BF16),
         ],
-        compiler_params=pltpu.CompilerParams(vmem_limit_bytes=VMEM),
+        compiler_params=pltpu.CompilerParams(vmem_limit_bytes=16 * 1024 * 1024),
         cost_estimate=pl.CostEstimate(
             flops=4 * sources * units * cap * cap, bytes_accessed=8 * sources * units * cap, transcendentals=0
         ),
@@ -174,7 +181,7 @@
             pltpu.VMEM((sources, width, cap), BF16),
             pltpu.SemaphoreType.DMA((sources // STEP, 2)),
         ],
-        compiler_params=pltpu.CompilerParams(vmem_limit_bytes=VMEM),
+        compiler_params=pltpu.CompilerParams(vmem_limit_bytes=50 * 1024 * 1024),
         cost_estimate=pl.CostEstimate(
             flops=2 * sources * width * cap, bytes_accessed=4 * sources * width * cap, transcendentals=0
         ),
@@ -196,7 +203,7 @@
             pl.BlockSpec(memory_space=pl.ANY),
             pl.BlockSpec(memory_space=pl.ANY),
         ],
-        out_specs=pl.BlockSpec(memory_space=pltpu.VMEM),
+        out_specs=pl.BlockSpec(memory_space=pl.ANY),
         out_shape=jax.ShapeDtypeStruct((nx * nl, nh * size, LANE), BF16),
         scratch_shapes=[
             pltpu.VMEM((high, wide), F32),
@@ -204,9 +211,11 @@
             pltpu.VMEM((lines, LANE), F32),
             pltpu.VMEM((sources, cols, cap), BF16),
             pltpu.VMEM(hp.shape, BF16),
+            pltpu.VMEM((nx * nl, nh * size, LANE), BF16),
             pltpu.SemaphoreType.DMA((sources // STEP, STEP + 1)),
-        ],
-        compiler_params=pltpu.CompilerParams(vmem_limit_bytes=VMEM),
+            pltpu.SemaphoreType.DMA((nx * nl,)),
+        ],
+        compiler_params=pltpu.CompilerParams(vmem_limit_bytes=50 * 1024 * 1024),
         cost_estimate=pl.CostEstimate(
             flops=2 * sources * cap * high * wide, bytes_accessed=2 * sources * cols * cap, transcendentals=0
         ),
@@ -244,12 +253,13 @@
     second = lax.all_to_all(
         partial_sum.reshape(nh, -1, LANE), "zh", split_axis=0, concat_axis=0, tiled=True
     )
-    summed = jnp.sum(second.astype(F32), axis=0).astype(BF16)
-    weight_grad = summed.reshape(1, -1)[:, : units * cols // (nx * nh * nl)]
-
     returned = lax.dynamic_slice_in_dim(everyones, me, 1, axis=1)[:, 0, 0]
     combined = jnp.sum(returned.reshape(experts, split, cap), axis=1)
     router_grad = jnp.sum(jnp.where(names, combined[:, None, :], 0.0), axis=0).T
+    second, router_grad = lax.optimization_barrier((second, router_grad))
+
+    summed = jnp.sum(second.astype(F32), axis=0).astype(BF16)
+    weight_grad = summed.reshape(1, -1)[:, : units * cols // (nx * nh * nl)]
     return (weight_grad, router_grad)
 
 

time: 138 us -> 138 us (level)
  Pallas kernels: 14.8 us -> 12.1 us
  local copies, waits for them, and re-layouts: 2.71 us -> 4.85 us
    pallas_call x1, Pallas kernels: 5.3 us -> 2.47 us  [place(): pl.pallas_call(place_kernel, grid_spec=pltpu.PrefetchScalarGridSpec(num_s...]
    unnamed x5 -> x7, local copies, waits for them, and re-layouts: 1.25 us -> 3.39 us
  transfers between devices with their start and end apart: 4 -> 4, of which waited for: 4 -> 4; matrix products, arithmetic and copies ran while one was open for 4% -> 4% of each run, Pallas kernels for 9% -> 7%
where the time goes in v6:
time: 138 us; the launch traced here: 137 us
  waiting for transfers between devices  53.3 us (39%)
  starting transfers between devices  28.5 us (21%)
  blocking collectives  21.2 us (15%)
  between operations  14.1 us (10%)
  Pallas kernels  12.1 us (9%)
  local copies, waits for them, and re-layouts  4.85 us (4%)
  other arithmetic  3.49 us (3%)
    all_gather x1, waiting for transfers between devices, local(): gathered = lax.all_gather(out_grad.T, ('y', 'c'), axis=0)  32.5 us
    all_to_all x1, blocking collectives, local(): lax.all_to_all(term, ('x', 'zl'), split_axis=0, concat_axis=0, tiled=True)  21.2 us
    all_to_all x1, starting transfers between devices, local(): lax.all_to_all(sent, ('y', 'c'), split_axis=0, concat_axis=0, tiled=True)  16.4 us
    all_to_all x1, starting transfers between devices, local(): lax.all_to_all(partial_sum.reshape(nh, -1, LANE), 'zh', split_axis=0, con...  12 us
    all_to_all x1, waiting for transfers between devices, local(): lax.all_to_all(partial_sum.reshape(nh, -1, LANE), 'zh', split_axis=0, con...  8.17 us
    pallas_call x1, Pallas kernels, weight_term(): pl.pallas_call(functools.partial(term_kernel, shape), in_specs=[pl.BlockS...  7.18 us
    all_to_all x1, waiting for transfers between devices, local(): lax.all_to_all(sent, ('y', 'c'), split_axis=0, concat_axis=0, tiled=True)  6.22 us
    all_gather x1, waiting for transfers between devices, local(): everyones = lax.all_gather(scores, ('y', 'c'), axis=0)  5.65 us
  transfers between devices with their start and end apart: 4, of which 4 were waited for; matrix products, arithmetic and copies ran while one was open for 4% of the time, Pallas kernels for 7%

profile of v6, /device:TPU:8, one launch (start us, length us, event | category | flops | bytes accessed | tf_op | source)
XLA Modules:
  0.0 137.4 jit_solution(9608698812664809116)
XLA Ops:
  7.2 0.0 all-gather.5.cloned.1.call-start
  7.2 0.7 all-gather.5.cloned.1.call-update
  7.9 0.7 convert_bitcast_fusion
  8.6 0.7 convert_bitcast_fusion.1
  9.3 0.7 select_reduce_fusion.1
  10.0 0.6 broadcast_in_dim.39
  10.6 16.4 %all-to-all-start = ((f32[16,2,128]{2,1,0:T(2,128)}), f32[16,2,128]{2,1,0:T(2,128)S(1)}, u32[]{:S(2)}, u32[]{:S(2)}) async-start(f32[16,2,128]{2,1,0:T(2,128)} %bitcast.5), calls=%async_computation | async-start | bytes 32768 | tf_op jit(solution)/shard_map/all_to_all | solution.py:242
  27.0 0.0 all-gather.7.cloned.1.call-start
  27.0 6.2 %all-to-all-done.meta_ref = f32[16,2,128]{2,1,0:T(2,128)S(1)} async-done(((f32[16,2,128]{2,1,0:T(2,128)}), f32[16,2,128]{2,1,0:T(2,128)S(1)}, u32[]{:S(2)}, u32[]{:S(2)}) %all-to-all-start) | async-done | bytes 16416 | tf_op jit(solution)/shard_map/all_to_all | solution.py:242
  33.3 0.0 copy-start
  33.3 1.4 copy-done
  34.6 0.0 copy-start.1
  34.6 1.4 copy-done.1
  36.0 2.5 %shard_map.77 = (bf16[4,384,512]{2,1,0:T(8,128)(2,1)S(1)}, bf16[16,368,128]{2,1,0:T(8,128)(2,1)S(1)}) custom-call(s32[1]{0:T(128)} %bitcast.8.part_ref, f32[16,2,128]{2,1,0:T(2,128)S(1)} %all-to-all-done.meta_ref, bf16[16,360,128]{2,1,0:T(8,128)(2,1)S(1)} %bitcast.28, bf16[16,360,128]{2,1,0:T(8,128)(2,1)S(1)} %bitcast.29), custom_call_target="tpu_custom_call" | custom-call | flops 377487360 | bytes 5898240 | tf_op jit(solution)/shard_map/pallas_call | solution.py:142
  38.5 32.5 %all-gather.5.cloned.1.call-done = bf16[23040,128]{1,0:T(8,128)(2,1)} async-done(((bf16[1440,128]{1,0:T(8,128)(2,1)}), bf16[23040,128]{1,0:T(8,128)(2,1)}) %all-gather.5.cloned.1.call-update) | async-done | bytes 5898256 | tf_op jit(solution)/shard_map/all_gather | solution.py:236
  71.0 2.4 %shard_map.78 = f32[16,16,128]{2,1,0:T(8,128)} custom-call(s32[1]{0:T(128)} %bitcast.8.part_ref, bf16[16,1440,128]{2,1,0:T(8,128)(2,1)} %bitcast.30, bf16[16,368,128]{2,1,0:T(8,128)(2,1)S(1)} %get-tuple-element.8.op_ref), custom_call_target="tpu_custom_call" | custom-call | flops 1507328 | bytes 3014656 | tf_op jit(solution)/shard_map/pallas_call | solution.py:171
  73.4 0.0 all-gather.7.cloned.1.call-update
  73.5 7.2 %shard_map.79 = bf16[8,512,128]{2,1,0:T(8,128)(2,1)S(1)} custom-call(f32[16,2,128]{2,1,0:T(2,128)S(1)} %all-to-all-done.meta_ref, bf16[16,1440,128]{2,1,0:T(8,128)(2,1)} %bitcast.31, bf16[4,384,512]{2,1,0:T(8,128)(2,1)S(1)} %get-tuple-element.10.hp_ref), custom_call_target="tpu_custom_call" | custom-call | flops 2415919104 | bytes 5898240 | tf_op jit(solution)/shard_map/pallas_call | solution.py:199
  80.7 0.0 copy-start.2
  80.7 21.2 %all_to_all.15 = bf16[8,512,128]{2,1,0:T(8,128)(2,1)S(1)} all-to-all(bf16[8,512,128]{2,1,0:T(8,128)(2,1)S(1)} %shard_map.79), channel_id=1, replica_groups=mesh['x'=4,'zh'=8,'zl'=2,'y'=8,'c'=2] {'x','zl'}, dimensions={0} | all-to-all | bytes 2097152 | tf_op jit(solution)/shard_map/all_to_all | solution.py:251
  101.9 0.8 reduce_sum.62
  102.7 12.0 %all-to-all-start.2 = ((bf16[8,64,128]{2,1,0:T(8,128)(2,1)}), bf16[8,64,128]{2,1,0:T(8,128)(2,1)S(1)}, u32[]{:S(2)}, u32[]{:S(2)}) async-start(bf16[8,64,128]{2,1,0:T(8,128)(2,1)} %bitcast.13), calls=%async_computation.2 | async-start | bytes 262144 | tf_op jit(solution)/shard_map/all_to_all | solution.py:253
  114.7 5.6 %all-gather.7.cloned.1.call-done = f32[256,16,128]{2,1,0:T(8,128)} async-done(((f32[16,16,128]{2,1,0:T(8,128)}), f32[256,16,128]{2,1,0:T(8,128)}) %all-gather.7.cloned.1.call-update) | async-done | bytes 2097168 | tf_op jit(solution)/shard_map/all_gather | solution.py:249
  120.3 0.8 constant_dynamic-slice_fusion
  121.2 0.0 copy-done.2
  121.2 0.6 fusion.2
  121.8 8.2 %all-to-all-done.2 = bf16[8,64,128]{2,1,0:T(8,128)(2,1)S(1)} async-done(((bf16[8,64,128]{2,1,0:T(8,128)(2,1)}), bf16[8,64,128]{2,1,0:T(8,128)(2,1)S(1)}, u32[]{:S(2)}, u32[]{:S(2)}) %all-to-all-start.2) | async-done | bytes 131104 | tf_op jit(solution)/shard_map/all_to_all | solution.py:253
  130.0 0.6 copy.11
  (3 shorter events, 0.0 us)
Async XLA Ops:
  7.2 63.9 %all-gather.5.cloned.1.call-start = ((), (), s32[]{:S(2)}) async-start(), calls=%async_computation.3 | async-start | bytes 6266880 | tf_op jit(solution)/shard_map/all_gather | solution.py:236
  10.6 22.7 %all-to-all-start = ((f32[16,2,128]{2,1,0:T(2,128)}), f32[16,2,128]{2,1,0:T(2,128)S(1)}, u32[]{:S(2)}, u32[]{:S(2)}) async-start(f32[16,2,128]{2,1,0:T(2,128)} %bitcast.5), calls=%async_computation | async-start | bytes 32768 | tf_op jit(solution)/shard_map/all_to_all | solution.py:242
  27.0 93.3 %all-gather.7.cloned.1.call-start = ((), (), s32[]{:S(2)}) async-start(), calls=%async_computation.4 | async-start | bytes 2228224 | tf_op jit(solution)/shard_map/all_gather | solution.py:249
  33.3 1.4 copy-start
  34.6 1.4 copy-start.1
  80.7 40.5 %copy-start.2 = (s32[128,4]{0,1:T(4,128)S(1)}, s32[128,4]{0,1:T(4,128)}, u32[]{:S(2)}) copy-start(s32[128,4]{0,1:T(4,128)} %param.7) | copy-start | bytes 6148
  102.7 27.3 %all-to-all-start.2 = ((bf16[8,64,128]{2,1,0:T(8,128)(2,1)}), bf16[8,64,128]{2,1,0:T(8,128)(2,1)S(1)}, u32[]{:S(2)}, u32[]{:S(2)}) async-start(bf16[8,64,128]{2,1,0:T(8,128)(2,1)} %bitcast.13), calls=%async_computation.2 | async-start | bytes 262144 | tf_op jit(solution)/shard_map/all_to_all | solution.py:253
Sparse Core Ops, SparseCore 0:
  10.7 60.2 all-gather.4
  73.7 46.5 all-gather.6

commit v7 on v5

--- a/solution.py
+++ b/solution.py
@@ -144,7 +144,7 @@
             jax.ShapeDtypeStruct((sources // STEP, FOLD * rows, STEP * cap), BF16),
             jax.ShapeDtypeStruct((sources, width, cap), BF16),
         ],
-        compiler_params=pltpu.CompilerParams(vmem_limit_bytes=VMEM),
+        compiler_params=pltpu.CompilerParams(vmem_limit_bytes=16 * 1024 * 1024),
         cost_estimate=pl.CostEstimate(
             flops=4 * sources * units * cap * cap, bytes_accessed=8 * sources * units * cap, transcendentals=0
         ),
@@ -187,7 +187,7 @@
             pltpu.SemaphoreType.DMA((sources // STEP, STEP + 2)),
             pltpu.SemaphoreType.DMA((nx * nl,)),
         ],
-        compiler_params=pltpu.CompilerParams(vmem_limit_bytes=VMEM),
+        compiler_params=pltpu.CompilerParams(vmem_limit_bytes=46 * 1024 * 1024),
         cost_estimate=pl.CostEstimate(
             flops=2 * sources * cap * high * wide, bytes_accessed=2 * sources * cols * cap, transcendentals=0
         ),

time: 137 us -> 138 us (level)
  local copies, waits for them, and re-layouts: 2.71 us -> 5.83 us
  Pallas kernels: 13.5 us -> 10.8 us
    unnamed x5 -> x9, local copies, waits for them, and re-layouts: 1.25 us -> 4.37 us
    pallas_call x1, Pallas kernels: 5.28 us -> 2.47 us  [place(): pl.pallas_call(place_kernel, grid_spec=pltpu.PrefetchScalarGridSpec(num_s...]
  transfers between devices with their start and end apart: 4 -> 4, of which waited for: 4 -> 4; matrix products, arithmetic and copies ran while one was open for 4% -> 4% of each run, Pallas kernels for 4% -> 2%
where the time goes in v7:
time: 138 us
  waiting for transfers between devices  53.3 us (39%)
  starting transfers between devices  28.5 us (21%)
  blocking collectives  21.5 us (16%)
  between operations  14.1 us (10%)
  Pallas kernels  10.8 us (8%)
  local copies, waits for them, and re-layouts  5.83 us (4%)
  other arithmetic  3.5 us (3%)
    all_gather x1, waiting for transfers between devices, local(): gathered = lax.all_gather(out_grad.T, ('y', 'c'), axis=0)  32.5 us
    all_to_all x1, blocking collectives, local(): lax.all_to_all(term, ('x', 'zl'), split_axis=0, concat_axis=0, tiled=True)  21.5 us
    all_to_all x1, starting transfers between devices, local(): lax.all_to_all(sent, ('y', 'c'), split_axis=0, concat_axis=0, tiled=True)  16.4 us
    all_gather x1, waiting for transfers between devices, local(): everyones = lax.all_gather(scores, ('y', 'c'), axis=0)  12.8 us
    all_to_all x1, starting transfers between devices, local(): lax.all_to_all(partial_sum.reshape(nh, -1, LANE), 'zh', split_axis=0, con...  12 us
    pallas_call x1, Pallas kernels, weight_term(): pl.pallas_call(functools.partial(term_kernel, shape), in_specs=[pl.BlockS...  8.37 us
    all_to_all x1, waiting for transfers between devices, local(): lax.all_to_all(sent, ('y', 'c'), split_axis=0, concat_axis=0, tiled=True)  6.22 us
    unnamed x9, local copies, waits for them, and re-layouts  4.37 us
  transfers between devices with their start and end apart: 4, of which 4 were waited for; matrix products, arithmetic and copies ran while one was open for 4% of the time, Pallas kernels for 2%

profile of v7, /device:TPU:8, one launch (start us, length us, event | category | flops | bytes accessed | tf_op | source)
XLA Modules:
  0.0 137.6 jit_solution(9749879201850674407)
XLA Ops:
  7.2 0.0 all-gather.5.cloned.1.call-start
  7.2 0.7 all-gather.5.cloned.1.call-update
  7.9 0.7 convert_bitcast_fusion
  8.6 0.7 convert_bitcast_fusion.1
  9.3 0.7 select_reduce_fusion.1
  10.0 0.6 broadcast_in_dim.39
  10.6 16.4 %all-to-all-start = ((f32[16,2,128]{2,1,0:T(2,128)}), f32[16,2,128]{2,1,0:T(2,128)S(1)}, u32[]{:S(2)}, u32[]{:S(2)}) async-start(f32[16,2,128]{2,1,0:T(2,128)} %bitcast.6), calls=%async_computation | async-start | bytes 32768 | tf_op jit(solution)/shard_map/all_to_all | solution.py:214
  27.0 0.0 all-gather.7.cloned.1.call-start
  27.0 6.2 %all-to-all-done.meta_ref = f32[16,2,128]{2,1,0:T(2,128)S(1)} async-done(((f32[16,2,128]{2,1,0:T(2,128)}), f32[16,2,128]{2,1,0:T(2,128)S(1)}, u32[]{:S(2)}, u32[]{:S(2)}) %all-to-all-start) | async-done | bytes 16416 | tf_op jit(solution)/shard_map/all_to_all | solution.py:214
  33.3 0.0 copy-start
  33.3 1.4 copy-done
  34.6 0.0 copy-start.1
  34.6 1.4 copy-done.1
  36.0 2.5 %shard_map.77 = (bf16[4,384,512]{2,1,0:T(8,128)(2,1)S(1)}, bf16[16,368,128]{2,1,0:T(8,128)(2,1)S(1)}) custom-call(s32[1]{0:T(128)} %bitcast.part_ref, f32[16,2,128]{2,1,0:T(2,128)S(1)} %all-to-all-done.meta_ref, bf16[16,360,128]{2,1,0:T(8,128)(2,1)S(1)} %bitcast.28, bf16[16,360,128]{2,1,0:T(8,128)(2,1)S(1)} %bitcast.29), custom_call_target="tpu_custom_call" | custom-call | flops 377487360 | bytes 5898240 | tf_op jit(solution)/shard_map/pallas_call | solution.py:127
  38.5 32.5 %all-gather.5.cloned.1.call-done = bf16[23040,128]{1,0:T(8,128)(2,1)} async-done(((bf16[1440,128]{1,0:T(8,128)(2,1)}), bf16[23040,128]{1,0:T(8,128)(2,1)}) %all-gather.5.cloned.1.call-update) | async-done | bytes 5898256 | tf_op jit(solution)/shard_map/all_gather | solution.py:208
  71.0 8.4 %shard_map.78 = (bf16[8,512,128]{2,1,0:T(8,128)(2,1)S(1)}, f32[16,16,128]{2,1,0:T(8,128)}) custom-call(s32[1]{0:T(128)} %bitcast.part_ref, f32[16,2,128]{2,1,0:T(2,128)S(1)} %all-to-all-done.meta_ref, bf16[16,1440,128]{2,1,0:T(8,128)(2,1)} %bitcast.30, bf16[4,384,512]{2,1,0:T(8,128)(2,1)S(1)} %get-tuple-element.8.hp_ref, ...), custom_call_target="tpu_custom_call" | custom-call | flops 2415919104 | bytes 5898240 | tf_op jit(solution)/shard_map/pallas_call | solution.py:162
  79.4 0.0 copy-start.2
  79.4 1.0 copy-done.2
  80.4 0.0 all-gather.7.cloned.1.call-update
  80.4 0.0 copy-start.3
  80.4 21.5 %all_to_all.15 = bf16[8,512,128]{2,1,0:T(8,128)(2,1)S(1)} all-to-all(bf16[8,512,128]{2,1,0:T(8,128)(2,1)} %copy-done.2), channel_id=1, replica_groups=mesh['x'=4,'zh'=8,'zl'=2,'y'=8,'c'=2] {'x','zl'}, dimensions={0} | all-to-all | bytes 2097152 | tf_op jit(solution)/shard_map/all_to_all | solution.py:222
  101.9 0.8 reduce_sum.62
  102.7 12.0 %all-to-all-start.2 = ((bf16[8,64,128]{2,1,0:T(8,128)(2,1)}), bf16[8,64,128]{2,1,0:T(8,128)(2,1)S(1)}, u32[]{:S(2)}, u32[]{:S(2)}) async-start(bf16[8,64,128]{2,1,0:T(8,128)(2,1)} %bitcast.13), calls=%async_computation.2 | async-start | bytes 262144 | tf_op jit(solution)/shard_map/all_to_all | solution.py:224
  114.7 12.8 %all-gather.7.cloned.1.call-done = f32[256,16,128]{2,1,0:T(8,128)} async-done(((f32[16,16,128]{2,1,0:T(8,128)}), f32[256,16,128]{2,1,0:T(8,128)}) %all-gather.7.cloned.1.call-update) | async-done | bytes 2097168 | tf_op jit(solution)/shard_map/all_gather | solution.py:220
  127.5 0.8 constant_dynamic-slice_fusion
  128.4 0.0 copy-done.3
  128.4 0.6 fusion.2
  129.0 1.1 all-to-all-done.2
  130.1 0.6 copy.11
  (3 shorter events, 0.0 us)
Async XLA Ops:
  7.2 63.9 %all-gather.5.cloned.1.call-start = ((), (), s32[]{:S(2)}) async-start(), calls=%async_computation.3 | async-start | bytes 6266880 | tf_op jit(solution)/shard_map/all_gather | solution.py:208
  10.6 22.7 %all-to-all-start = ((f32[16,2,128]{2,1,0:T(2,128)}), f32[16,2,128]{2,1,0:T(2,128)S(1)}, u32[]{:S(2)}, u32[]{:S(2)}) async-start(f32[16,2,128]{2,1,0:T(2,128)} %bitcast.6), calls=%async_computation | async-start | bytes 32768 | tf_op jit(solution)/shard_map/all_to_all | solution.py:214
  27.0 100.5 %all-gather.7.cloned.1.call-start = ((), (), s32[]{:S(2)}) async-start(), calls=%async_computation.4 | async-start | bytes 2228224 | tf_op jit(solution)/shard_map/all_gather | solution.py:220
  33.3 1.4 copy-start
  34.6 1.4 copy-start.1
  79.4 1.0 copy-start.2
  80.4 48.0 %copy-start.3 = (s32[128,4]{0,1:T(4,128)S(1)}, s32[128,4]{0,1:T(4,128)}, u32[]{:S(2)}) copy-start(s32[128,4]{0,1:T(4,128)} %param.7) | copy-start | bytes 6148
  102.7 27.4 %all-to-all-start.2 = ((bf16[8,64,128]{2,1,0:T(8,128)(2,1)}), bf16[8,64,128]{2,1,0:T(8,128)(2,1)S(1)}, u32[]{:S(2)}, u32[]{:S(2)}) async-start(bf16[8,64,128]{2,1,0:T(8,128)(2,1)} %bitcast.13), calls=%async_computation.2 | async-start | bytes 262144 | tf_op jit(solution)/shard_map/all_to_all | solution.py:224
Sparse Core Ops, SparseCore 0:
  10.7 60.2 all-gather.4
  80.5 46.9 all-gather.6

commit v8 on v5

--- a/solution.py
+++ b/solution.py
@@ -73,7 +73,7 @@
             window = grads[j, pl.ds(start, width), :].astype(F32)
             score = jnp.sum(out[j].astype(F32) * window, axis=0, keepdims=True)
             s_ref[j] = jnp.broadcast_to(score, s_ref.shape[1:])
-            rhs[:cols, u * cap : (u + 1) * cap] = (grads[j].astype(F32) * weight).astype(BF16)
+            rhs[:cols, u * cap : (u + 1) * cap] = grads[j] * weight.astype(BF16)
         for n in range(0, wide, TILE):
             term = lax.dot_general(
                 hidden[i],

time: 137 us -> 137 us (level)
  no operation moved by 1% of the time
where the time goes in v8:
time: 137 us; the launch traced here: 136 us
  waiting for transfers between devices  52.6 us (38%)
  starting transfers between devices  28.6 us (21%)
  blocking collectives  21.4 us (16%)
  between operations  14.1 us (10%)
  Pallas kernels  13.3 us (10%)
  other arithmetic  3.5 us (3%)
  local copies, waits for them, and re-layouts  2.71 us (2%)
    all_gather x1, waiting for transfers between devices, local(): gathered = lax.all_gather(out_grad.T, ('y', 'c'), axis=0)  31.9 us
    all_to_all x1, blocking collectives, local(): lax.all_to_all(term, ('x', 'zl'), split_axis=0, concat_axis=0, tiled=True)  21.4 us
    all_to_all x1, starting transfers between devices, local(): lax.all_to_all(sent, ('y', 'c'), split_axis=0, concat_axis=0, tiled=True)  16.4 us
    all_gather x1, waiting for transfers between devices, local(): everyones = lax.all_gather(scores, ('y', 'c'), axis=0)  12.8 us
    all_to_all x1, starting transfers between devices, local(): lax.all_to_all(partial_sum.reshape(nh, -1, LANE), 'zh', split_axis=0, con...  12.1 us
    pallas_call x1, Pallas kernels, weight_term(): pl.pallas_call(functools.partial(term_kernel, shape), in_specs=[pl.BlockS...  8.06 us
    all_to_all x1, waiting for transfers between devices, local(): lax.all_to_all(sent, ('y', 'c'), split_axis=0, concat_axis=0, tiled=True)  6.22 us
    pallas_call x1, Pallas kernels, place(): pl.pallas_call(place_kernel, grid_spec=pltpu.PrefetchScalarGridSpec(num_s...  5.28 us
  transfers between devices with their start and end apart: 4, of which 4 were waited for; matrix products, arithmetic and copies ran while one was open for 4% of the time, Pallas kernels for 4%

profile of v8, /device:TPU:8, one launch (start us, length us, event | category | flops | bytes accessed | tf_op | source)
XLA Modules:
  0.0 136.2 jit_solution(9494888114029025558)
XLA Ops:
  7.2 0.0 all-gather.5.cloned.1.call-start
  7.2 0.7 all-gather.5.cloned.1.call-update
  7.9 0.7 convert_bitcast_fusion
  8.6 0.7 convert_bitcast_fusion.1
  9.3 0.7 select_reduce_fusion.1
  10.0 0.6 broadcast_in_dim.39
  10.6 16.4 %all-to-all-start = ((f32[16,2,128]{2,1,0:T(2,128)}), f32[16,2,128]{2,1,0:T(2,128)S(1)}, u32[]{:S(2)}, u32[]{:S(2)}) async-start(f32[16,2,128]{2,1,0:T(2,128)} %bitcast.6), calls=%async_computation | async-start | bytes 32768 | tf_op jit(solution)/shard_map/all_to_all | solution.py:214
  27.0 0.0 all-gather.7.cloned.1.call-start
  27.0 6.2 %all-to-all-done.meta_ref = f32[16,2,128]{2,1,0:T(2,128)S(1)} async-done(((f32[16,2,128]{2,1,0:T(2,128)}), f32[16,2,128]{2,1,0:T(2,128)S(1)}, u32[]{:S(2)}, u32[]{:S(2)}) %all-to-all-start) | async-done | bytes 16416 | tf_op jit(solution)/shard_map/all_to_all | solution.py:214
  33.3 0.0 copy-start
  33.3 0.6 copy-done
  33.9 5.3 %shard_map.77 = (bf16[4,384,512]{2,1,0:T(8,128)(2,1)}, bf16[16,368,128]{2,1,0:T(8,128)(2,1)}) custom-call(s32[1]{0:T(128)} %bitcast.part_ref, f32[16,2,128]{2,1,0:T(2,128)} %copy-done, bf16[16,360,128]{2,1,0:T(8,128)(2,1)} %bitcast.29, bf16[16,360,128]{2,1,0:T(8,128)(2,1)} %bitcast.30), custom_call_target="tpu_custom_call" | custom-call | flops 377487360 | bytes 5898240 | tf_op jit(solution)/shard_map/pallas_call | solution.py:127
  39.2 31.9 %all-gather.5.cloned.1.call-done = bf16[23040,128]{1,0:T(8,128)(2,1)} async-done(((bf16[1440,128]{1,0:T(8,128)(2,1)}), bf16[23040,128]{1,0:T(8,128)(2,1)}) %all-gather.5.cloned.1.call-update) | async-done | bytes 5898256 | tf_op jit(solution)/shard_map/all_gather | solution.py:208
  71.0 8.1 %shard_map.78 = (bf16[8,512,128]{2,1,0:T(8,128)(2,1)}, f32[16,16,128]{2,1,0:T(8,128)}) custom-call(s32[1]{0:T(128)} %bitcast.part_ref, f32[16,2,128]{2,1,0:T(2,128)} %copy-done, bf16[16,1440,128]{2,1,0:T(8,128)(2,1)} %bitcast.28, bf16[4,384,512]{2,1,0:T(8,128)(2,1)} %get-tuple-element.8.hp_ref, bf16[16,368,128]{2,1,0:T(8,128)(2,1)} %get-tuple-element.9.op_ref), custom_call_target="tpu_custom_call" | custom-call | flops 2415919104 | bytes 5898240 | tf_op jit(solution)/shard_map/pallas_call | solution.py:162
  79.1 0.0 all-gather.7.cloned.1.call-update
  79.1 0.0 copy-start.1
  79.1 21.4 %all_to_all.15 = bf16[8,512,128]{2,1,0:T(8,128)(2,1)S(1)} all-to-all(bf16[8,512,128]{2,1,0:T(8,128)(2,1)} %get-tuple-element.10), channel_id=1, replica_groups=mesh['x'=4,'zh'=8,'zl'=2,'y'=8,'c'=2] {'x','zl'}, dimensions={0} | all-to-all | bytes 2097152 | tf_op jit(solution)/shard_map/all_to_all | solution.py:222
  100.5 0.8 reduce_sum.62
  101.3 12.1 %all-to-all-start.2 = ((bf16[8,64,128]{2,1,0:T(8,128)(2,1)}), bf16[8,64,128]{2,1,0:T(8,128)(2,1)S(1)}, u32[]{:S(2)}, u32[]{:S(2)}) async-start(bf16[8,64,128]{2,1,0:T(8,128)(2,1)} %bitcast.13), calls=%async_computation.2 | async-start | bytes 262144 | tf_op jit(solution)/shard_map/all_to_all | solution.py:224
  113.4 12.8 %all-gather.7.cloned.1.call-done = f32[256,16,128]{2,1,0:T(8,128)} async-done(((f32[16,16,128]{2,1,0:T(8,128)}), f32[256,16,128]{2,1,0:T(8,128)}) %all-gather.7.cloned.1.call-update) | async-done | bytes 2097168 | tf_op jit(solution)/shard_map/all_gather | solution.py:220
  126.2 0.8 constant_dynamic-slice_fusion
  127.1 0.0 copy-done.1
  127.1 0.6 fusion.2
  127.7 1.1 all-to-all-done.2
  128.8 0.6 copy.11
  (3 shorter events, 0.0 us)
Async XLA Ops:
  7.2 63.9 %all-gather.5.cloned.1.call-start = ((), (), s32[]{:S(2)}) async-start(), calls=%async_computation.3 | async-start | bytes 6266880 | tf_op jit(solution)/shard_map/all_gather | solution.py:208
  10.6 22.7 %all-to-all-start = ((f32[16,2,128]{2,1,0:T(2,128)}), f32[16,2,128]{2,1,0:T(2,128)S(1)}, u32[]{:S(2)}, u32[]{:S(2)}) async-start(f32[16,2,128]{2,1,0:T(2,128)} %bitcast.6), calls=%async_computation | async-start | bytes 32768 | tf_op jit(solution)/shard_map/all_to_all | solution.py:214
  27.0 99.2 %all-gather.7.cloned.1.call-start = ((), (), s32[]{:S(2)}) async-start(), calls=%async_computation.4 | async-start | bytes 2228224 | tf_op jit(solution)/shard_map/all_gather | solution.py:220
  33.3 0.6 copy-start
  79.1 48.0 %copy-start.1 = (s32[128,4]{0,1:T(4,128)S(1)}, s32[128,4]{0,1:T(4,128)}, u32[]{:S(2)}) copy-start(s32[128,4]{0,1:T(4,128)} %param.7) | copy-start | bytes 6148
  101.3 27.4 %all-to-all-start.2 = ((bf16[8,64,128]{2,1,0:T(8,128)(2,1)}), bf16[8,64,128]{2,1,0:T(8,128)(2,1)S(1)}, u32[]{:S(2)}, u32[]{:S(2)}) async-start(bf16[8,64,128]{2,1,0:T(8,128)(2,1)} %bitcast.13), calls=%async_computation.2 | async-start | bytes 262144 | tf_op jit(solution)/shard_map/all_to_all | solution.py:224
Sparse Core Ops, SparseCore 0:
  10.7 60.2 all-gather.4
  79.2 46.9 all-gather.6
